TPU v7x, 256 devices: a whole 4x4x8 slice. The times are simulated.
256 devices in a mesh: blk: 128 (over x, z, y_hi, core), half: 2 (over y_lo).
Axes of the slice: x: 4, y: 4 (y_hi: 2, y_lo: 2; y = y_hi * 2 + y_lo), z: 8, core: 2. Of those that a mesh axis runs over, the one named last changes fastest.
Arguments:
- points: float32 [32, 393216], P(None, ('blk', 'half')), may hold values from -6 to 6
- vectors: float32 [17, 393216], P(None, ('blk', 'half')), may hold values from -6 to 6
- inv_length: float32 [32], replicated, may hold values from 0.12 to 0.35
- signal_var: float32 [1], replicated, may hold values from 0.02 to 0.1
- noise_var: float32 [1], replicated, may hold values from 0.05 to 0.5
- masks: int32 [3], replicated, may hold values from 1 to 127, as said below
Outputs:
- product: float32 [17, 393216], P(None, ('blk', 'half'))
Inputs may be any that keep to these rules, and one draw needn't show every extreme that they name: `masks`: the entries are distinct; one of them is 1 and one is 127.
All inputs are finite; a program needn't handle non-finite values.
Results may differ from a plain program's by a relative error of at most 0.0003.
Values sent between devices are 32-bit elements; how exact they have to be, the bound alone decides.
A program may use at most 64 MiB of HBM per device.

v0:
```python
import functools
import math

import jax
import jax.numpy as jnp
import numpy as np
from jax import lax
from jax.experimental import pallas as pl
from jax.experimental.pallas import tpu as pltpu
from jax.sharding import PartitionSpec as P

F32 = jnp.float32
BF16 = jnp.bfloat16
LOW = jnp.float8_e5m2
LOG2E = math.log2(math.e)
ALPHA = 1.5 * LOG2E
BETA = 0.75 * LOG2E * LOG2E
FACTOR = math.exp(1.5) / (3.0 * LOG2E * LOG2E)
STRETCH = math.sqrt(5.0) * LOG2E
TINY = 1e-30
DEPTH = 256
COLUMNS = 256


def pieces(x, count):
    out = []
    for _ in range(count):
        part = x.astype(BF16).astype(F32)
        out.append(part)
        x = x - part
    return out


def features(points, inv):
    x = points * inv
    norm = jnp.sum(x * x, axis=0, keepdims=True)
    return pieces(x, 3), pieces(norm, 3)


def row_side(points, inv):
    (h, m, l), norm = features(points, inv)
    one = jnp.ones_like(norm[0])
    tail = jnp.concatenate(norm + [one, one, one], axis=0)
    rest = jnp.zeros((DEPTH - 198, points.shape[1]), F32)
    return jnp.concatenate([-2.0 * p for p in (h, h, m, h, l, m)] + [tail, rest], axis=0).astype(BF16)


def column_side(points, inv):
    (h, m, l), norm = features(points, inv)
    one = jnp.ones_like(norm[0])
    tail = jnp.concatenate([one, one, one] + norm, axis=0)
    rest = jnp.zeros((DEPTH - 198, points.shape[1]), F32)
    return jnp.concatenate([h, m, h, l, h, m, tail, rest], axis=0).astype(BF16)


def vector_side(vectors):
    pad = jnp.zeros((7, vectors.shape[1]), F32)
    hi, lo = pieces(vectors, 2)
    wide = jnp.concatenate([hi, pad, lo, pad], axis=0).astype(BF16)
    first = vectors.astype(LOW).astype(F32)
    second = vectors - first
    fill = jnp.zeros((16, vectors.shape[1]), F32)
    low = jnp.concatenate([first, pad, second, pad, fill], axis=0).astype(LOW)
    return wide, low


def kernel_values(squared):
    q = jnp.maximum(squared, TINY)
    h = -ALPHA - q * lax.rsqrt(q)
    values = (h * h + BETA) * jnp.exp2(h)
    hi = values.astype(BF16)
    return hi, (values - hi.astype(F32)).astype(LOW)


def dot(a, b):
    return jnp.dot(a, b, preferred_element_type=F32)


def dot_t(a, b):
    return lax.dot_general(a, b, (((1,), (1,)), ((), ())), preferred_element_type=F32)


def folded(wide, low):
    return wide[0:24] + wide[24:48] + low[0:24] + low[24:48]


def column_step(i):
    return pl.ds(pl.multiple_of(i * COLUMNS, COLUMNS), COLUMNS)


def by_columns(n, step):
    def run(i, carry):
        step(pl.ds(pl.multiple_of(i * COLUMNS, COLUMNS), COLUMNS))
        return carry

    lax.fori_loop(0, n // COLUMNS, run, 0)


def one_way_body(source, mine, inv, base, out, rows, cols, vec, vec_low):
    n = mine.shape[1]

    def prepare(c):
        rows[c, :] = row_side(source[0:32, c], inv[...]).T
        cols[:, c] = column_side(mine[0:32, c], inv[...])
        vec[:, c], vec_low[:, c] = vector_side(source[32:49, c])

    def step(c):
        hi, lo = kernel_values(dot(rows[...], cols[:, c]))
        out[:, c] = base[:, c] + folded(dot(vec[...], hi), dot(vec_low[...], lo))[0:17]

    by_columns(n, prepare)
    by_columns(n, step)


def two_way_body(core, mine, sibling, other, inv, near, base, own, for_sibling, par, *scratch, count):
    rows, cols, vec_r, low_r, vec_c, low_c, acc, acc_low = scratch
    n = mine.shape[1]
    par[...] = jnp.zeros_like(par)

    def prepare_columns(c):
        cols[:, c] = column_side(other[0:32, c], inv[...])
        vec_c[:, c], low_c[:, c] = vector_side(other[32:49, c])

    by_columns(n, prepare_columns)

    def tile(k, carry):
        second = (core[0] if count == 1 else k) == 1

        def prepare_rows(c):
            side = jnp.where(second, sibling[:, c], mine[:, c])
            rows[c, :] = row_side(side[0:32, :], inv[...]).T
            vec_r[:, c], low_r[:, c] = vector_side(side[32:49, :])

        def step(c):
            hi, lo = kernel_values(dot(rows[...], cols[:, c]))
            par[:, c] += folded(dot(vec_r[...], hi), dot(low_r[...], lo))[0:17]
            acc[...] += dot_t(vec_c[:, c], hi)
            acc_low[...] += dot_t(low_c[:, c], lo)

        by_columns(n, prepare_rows)
        acc[...] = jnp.zeros_like(acc)
        acc_low[...] = jnp.zeros_like(acc_low)
        by_columns(n, step)
        total = folded(acc[...], acc_low[...])[0:17]
        if count == 1:
            own[...] = base[...] + jnp.where(second, 0.0, total)
            for_sibling[...] = near[...] + jnp.where(second, total, 0.0)
        else:

            @pl.when(k == 0)
            def _():
                own[...] = base[...] + total

            @pl.when(k == 1)
            def _():
                for_sibling[...] = near[...] + total

        return carry

    lax.fori_loop(0, count, tile, 0)


def operands(n):
    return [
        pltpu.VMEM((n, DEPTH), BF16),
        pltpu.VMEM((DEPTH, n), BF16),
        pltpu.VMEM((48, n), BF16),
        pltpu.VMEM((64, n), LOW),
    ]


def estimate(n, passes):
    return pl.CostEstimate(flops=2 * n * n * 256 * passes, bytes_accessed=4 * 115 * n, transcendentals=2 * n * n)


def tile_call(body, outs, passes, core, *arrays):
    n = arrays[0].shape[1]
    whole = pl.BlockSpec(memory_space=pltpu.VMEM)
    scratch = operands(n)
    if core is not None:
        scratch += [
            pltpu.VMEM((48, n), BF16),
            pltpu.VMEM((64, n), LOW),
            pltpu.VMEM((48, n), F32),
            pltpu.VMEM((64, n), F32),
        ]
        arrays = (core,) + arrays
    specs = [whole] * len(arrays)
    if core is not None:
        specs[0] = pl.BlockSpec(memory_space=pltpu.SMEM)
    return pl.pallas_call(
        body,
        out_shape=(jax.ShapeDtypeStruct((17, n), F32),) * outs,
        in_specs=specs,
        scratch_shapes=scratch,
        cost_estimate=estimate(n, passes),
        compiler_params=pltpu.CompilerParams(vmem_limit_bytes=48 << 20),
    )(*arrays)


AXES = ("blk", "half")
MESH = pl.DeviceIdType.MESH


def exchange_body(there, back, got, returned, sems, *, route):
    mask, last, kind = route
    block, half = lax.axis_index("blk"), lax.axis_index("half")
    bits = {k: lax.rem(lax.div(block, 1 << k), 2) for k in range(last.bit_length()) if (mask | kind) >> k & 1}
    one = block + mask - sum(bits[k] * (2 << k) for k in bits if mask >> k & 1)
    two = last - block
    change = lax.rem(sum(bits[k] for k in bits if kind >> k & 1), 2) * (two - one)
    ways = (one + change, half), (two - change, half)
    barrier = pltpu.get_barrier_semaphore()
    for device in ways:
        pl.semaphore_signal(barrier, inc=1, device_id=device, device_id_type=MESH)
    pl.semaphore_wait(barrier, 2)
    copies = [
        pltpu.make_async_remote_copy(
            src_ref=source,
            dst_ref=target,
            send_sem=sems.at[0, k],
            recv_sem=sems.at[1, k],
            device_id=device,
            device_id_type=MESH,
        )
        for k, (source, target, device) in enumerate(((there, got, ways[0]), (back, returned, ways[1])))
    ]
    for copy in copies:
        copy.start()
    for copy in copies:
        copy.wait()


def exchange(there, back, route, number):
    hbm = pl.BlockSpec(memory_space=pl.ANY)
    return pl.pallas_call(
        functools.partial(exchange_body, route=route),
        out_shape=(jax.ShapeDtypeStruct(there.shape, F32), jax.ShapeDtypeStruct(back.shape, F32)),
        in_specs=[hbm] * 2,
        out_specs=(hbm,) * 2,
        scratch_shapes=[pltpu.SemaphoreType.DMA((2, 2))],
        compiler_params=pltpu.CompilerParams(collective_id=number, has_side_effects=True),
    )(there, back)


def hops(size, start, flip):
    away = ((start ^ flip) - start) % size
    ways = []
    if away and 2 * away <= size:
        ways.append((0, [(start + k) % size for k in range(away)], 0.5 if 2 * away == size else 1.0))
    if away and 2 * away >= size:
        ways.append((1, [(start - k) % size for k in range(size - away)], 0.5 if 2 * away == size else 1.0))
    return ways


RINGS = ((4, 5, 2), (8, 2, 3), (2, 1, 1))


def loads_of(mask, blocks):
    out = np.zeros((blocks, 3, 2, blocks), np.float32)
    for block in range(blocks):
        at = block
        for axis, (size, low, bits) in enumerate(RINGS):
            field = ((1 << bits) - 1) << low
            for way, places, share in hops(size, (at & field) >> low, (mask & field) >> low):
                for place in places:
                    out[block, axis, way, ((at & ~field) | (place << low)) & ~1] += share
            at = (at & ~field) | ((block ^ mask) & field)
    return out.reshape(blocks, -1)


def parity(x):
    return bin(x).count("1") & 1


def mate_routes(blocks):
    last = blocks - 1
    masks = range(4, blocks, 4)
    loads = {m: loads_of(m, blocks) for m in [*masks, last]}
    kinds = np.array([[parity(w & b) for b in range(blocks)] for w in range(blocks)], np.float32)
    routes = [(2, last, 2)]
    for mask in masks:
        worst = (kinds @ (loads[last] - loads[mask]) + loads[mask].sum(0)).max(1)
        fits = [w for w in range(0, blocks, 4) if parity(w & mask) and parity(w & last)]
        best = min(fits, key=lambda w: (round(float(worst[w]), 3), bin(w).count(str(1)), w))
        routes.append((mask, last, best))
    return routes


def local(points, vectors, inv_length, signal_var, noise_var, masks):
    inv = (inv_length * STRETCH)[:, None]
    mine = jnp.concatenate([points, vectors], axis=0)
    blocks = lax.axis_size("blk")
    last = blocks - 1
    middle = masks[0] ^ masks[1] ^ masks[2] ^ 1 ^ last
    which = middle >> 2
    routes = mate_routes(blocks)
    block = lax.axis_index("blk")
    core = (block & 1).reshape(1)
    kind = jnp.int32(0)
    for k in range(last.bit_length()):
        having = sum(1 << i for i, r in enumerate(routes) if r[2] >> k & 1)
        kind = kind ^ (np.uint32(having).astype(np.int32) >> which & block >> k & 1)
    lends = kind == 0
    lent_chip = lends & (middle & 1 == 1)
    lent_far = lends & (middle & 2 == 2) & (which > 0)

    chip = [(b, b ^ 1) for b in range(blocks)]
    apart = [(b, b ^ 2) for b in range(blocks)]
    swap = [(0, 1), (1, 0)]
    beside = lax.ppermute(mine, "blk", chip)
    sibling = lax.ppermute(mine, "half", swap)
    (own_self,) = tile_call(one_way_body, 1, 10, None, mine, mine, inv, jnp.zeros_like(vectors))
    beside, own_self = lax.optimization_barrier((beside, own_self))
    lent = jnp.where(lent_chip, beside, mine)
    across = lax.ppermute(lent, "blk", apart)
    zero = jnp.zeros_like(vectors)
    own, for_sibling, for_beside = tile_call(
        functools.partial(two_way_body, count=1), 3, 20, core, mine, sibling, beside, inv, zero, own_self
    )
    across, own = lax.optimization_barrier((across, own))
    sent = jnp.where(lent_far, across, lent)

    ways = [functools.partial(exchange, route=r, number=k) for k, r in enumerate(routes)]
    mate, _ = lax.switch(which, ways, sent, vectors)
    own, for_sibling, for_mate = tile_call(
        functools.partial(two_way_body, count=2), 3, 40, core, mine, sibling, mate, inv, for_sibling, own
    )
    from_sibling = lax.ppermute(for_sibling, "half", swap)
    _, returned = lax.switch(which, ways, mate, for_mate)
    from_across = lax.ppermute(jnp.where(lent_far, returned, 0.0), "blk", apart)
    (own,) = tile_call(one_way_body, 1, 10, None, sibling, mine, inv, own)
    kept = jnp.where(lent_far, 0.0, returned) + from_across
    from_beside = lax.ppermute(for_beside + jnp.where(lent_chip, kept, 0.0), "blk", chip)
    sums = own + from_sibling + from_beside + jnp.where(lent_chip, 0.0, kept)
    return (signal_var[0] * FACTOR) * sums + noise_var[0] * vectors


def solution(mesh):
    return jax.shard_map(
        local,
        mesh=mesh,
        in_specs=(P(None, AXES), P(None, AXES), P(), P(), P(), P()),
        out_specs=P(None, AXES),
        check_vma=False,
    )
```

profile of v0, /device:TPU:1, one launch (start us, length us, event | category | flops | bytes accessed | tf_op | source)
XLA Modules:
  0.0 106.5 jit_solution(17379300793653230995)
XLA Ops:
  0.0 1.0 constant_dynamic-update-slice_fusion.1
  1.0 0.0 copy-done
  1.0 2.2 %collective-permute-start = (f32[49,1536]{1,0:T(8,128)S(1)}, f32[49,1536]{1,0:T(8,128)S(1)}, u32[]{:S(2)}, u32[]{:S(2)}) collective-permute-start(f32[49,1536]{1,0:T(8,128)S(1)} %constant_dynamic-update-slice_fusion.source.mine), channel_id=1, source_target_pairs={{0,1},{1,0},{2,3},{3,2},{4,5},{5,4},{6,7},{7,6},{8,9},{9,8},{10,11... | collective-permute-start | bytes 903176 | tf_op jit(solution)/shard_map/ppermute | solution.py:312
  3.2 1.2 %collective-permute-start.1 = (f32[49,1536]{1,0:T(8,128)S(1)}, f32[49,1536]{1,0:T(8,128)S(1)}, u32[]{:S(2)}, u32[]{:S(2)}) collective-permute-start(f32[49,1536]{1,0:T(8,128)S(1)} %constant_dynamic-update-slice_fusion.source.mine), channel_id=1, source_target_pairs={{0,2},{2,0},{4,6},{6,4},{8,10},{10,8},{12,14},{14,12},{16,18},{18,... | collective-permute-start | bytes 903176 | tf_op jit(solution)/shard_map/ppermute | solution.py:311
  4.5 0.1 copy.10.inv
  4.6 6.9 %shard_map.64.base = f32[17,1536]{1,0:T(8,128)S(1)} custom-call(f32[49,1536]{1,0:T(8,128)S(1)} %constant_dynamic-update-slice_fusion.source.mine, f32[49,1536]{1,0:T(8,128)S(1)} %constant_dynamic-update-slice_fusion.source.mine, f32[32,1]{1,0:T(8,128)S(1)} %copy.10.inv, f32[17,1536]{1,0:T(8,128)S(1)} %broadcast_1_base_near.2.base.near), custom_call_target="tpu_custom_call" | custom-call | flops 12079595520 | bytes 706560 | tf_op jit(solution)/shard_map/pallas_call | solution.py:191
  11.5 0.0 copy-start.1
  11.5 0.6 copy-done.1
  12.1 0.7 fusion
  14.7 2.5 %collective-permute-start.2 = (f32[49,1536]{1,0:T(8,128)S(1)}, f32[49,1536]{1,0:T(8,128)S(1)}, u32[]{:S(2)}, u32[]{:S(2)}) collective-permute-start(f32[49,1536]{1,0:T(8,128)S(1)} %broadcast_select_fusion), channel_id=1, source_target_pairs={{0,4},{2,6},{4,0},{6,2},{8,12},{10,14},{12,8},{14,10},{16,20},{18,... | collective-permute-start | bytes 903176 | tf_op jit(solution)/shard_map/ppermute | solution.py:316
  17.2 0.0 collective-permute-done.sibling.source
  17.2 9.4 %shard_map.65 = (f32[17,1536]{1,0:T(8,128)S(1)}, f32[17,1536]{1,0:T(8,128)S(1)}, f32[17,1536]{1,0:T(8,128)S(1)}) custom-call(s32[1]{0:T(128)} %bitcast.2.core, f32[49,1536]{1,0:T(8,128)S(1)} %constant_dynamic-update-slice_fusion.source.mine, f32[49,1536]{1,0:T(8,128)S(1)} %collective-permute-done.sibling.source, ...), custom_call_target="tpu_custom_call" | custom-call | flops 24159191040 | bytes 706560 | tf_op jit(solution)/shard_map/pallas_call | solution.py:191
  26.6 24.5 %conditional.2 = (f32[49,1536]{1,0:T(8,128)S(1)}) conditional(s32[]{:T(128)} %bitcast.3, (f32[49,1536]{1,0:T(8,128)S(1)}, f32[17,1536]{1,0:T(8,128)S(1)}) %tuple.285, (f32[49,1536]{1,0:T(8,128)S(1)}, f32[17,1536]{1,0:T(8,128)S(1)}) %tuple.300, (f32[49,1536]{1,0:T(8,128)S(1)}, f32[17,1536]{1,0:T(8,128)S(1)}) %tuple.271, ...), branch_computations={%region_0.1_spmd, %region_1.2_spmd, %region_2.3_spmd, %region_3.4_... | conditional | bytes 8 | solution.py:325
  26.7 24.3 %branch_18_fun.2 = (f32[49,1536]{1,0:T(8,128)S(1)}, f32[17,1536]{1,0:T(8,128)}) custom-call(f32[49,1536]{1,0:T(8,128)S(1)} %get-tuple-element.373.there, f32[17,1536]{1,0:T(8,128)S(1)} %get-tuple-element.374.back), custom_call_target="tpu_custom_call" | custom-call | tf_op jit(solution)/shard_map/cond/branch_18_fun/pallas_call | solution.py:236
  51.2 18.3 %shard_map.66 = (f32[17,1536]{1,0:T(8,128)S(1)}, f32[17,1536]{1,0:T(8,128)S(1)}, f32[17,1536]{1,0:T(8,128)S(1)}) custom-call(s32[1]{0:T(128)} %bitcast.2.core, f32[49,1536]{1,0:T(8,128)S(1)} %constant_dynamic-update-slice_fusion.source.mine, f32[49,1536]{1,0:T(8,128)S(1)} %collective-permute-done.sibling.source, f32[49,1536]{1,0:T(8,128)S(1)} %get-tuple-element.542.other, ...), custom_call_target="tpu_custom_call" | custom-call | flops 48318382080 | bytes 706560 | tf_op jit(solution)/shard_map/pallas_call | solution.py:191
  69.5 21.0 %conditional.3 = (f32[17,1536]{1,0:T(8,128)S(1)}) conditional(s32[]{:T(128)} %bitcast.3, (f32[49,1536]{1,0:T(8,128)S(1)}, f32[17,1536]{1,0:T(8,128)S(1)}) %tuple.202, (f32[49,1536]{1,0:T(8,128)S(1)}, f32[17,1536]{1,0:T(8,128)S(1)}) %tuple.202, (f32[49,1536]{1,0:T(8,128)S(1)}, f32[17,1536]{1,0:T(8,128)S(1)}) %tuple.202, ...), branch_computations={%region_32.33_spmd, %region_33.34_spmd, %region_34.35_spmd, %regio... | conditional | bytes 8 | solution.py:330
  69.5 20.9 %branch_18_fun.3 = (f32[49,1536]{1,0:T(8,128)}, f32[17,1536]{1,0:T(8,128)S(1)}) custom-call(f32[49,1536]{1,0:T(8,128)S(1)} %get-tuple-element.477.there, f32[17,1536]{1,0:T(8,128)S(1)} %get-tuple-element.478.back), custom_call_target="tpu_custom_call" | custom-call | tf_op jit(solution)/shard_map/cond/branch_18_fun/pallas_call | solution.py:236
  90.5 1.5 %collective-permute-start.4 = (f32[17,1536]{1,0:T(8,128)S(1)}, f32[17,1536]{1,0:T(8,128)S(1)}, u32[]{:S(2)}, u32[]{:S(2)}) collective-permute-start(f32[17,1536]{1,0:T(8,128)S(1)} %broadcast_select_fusion.2), channel_id=1, source_target_pairs={{0,4},{2,6},{4,0},{6,2},{8,12},{10,14},{12,8},{14,10},{16,20},{18,... | collective-permute-start | bytes 313352 | tf_op jit(solution)/shard_map/ppermute | solution.py:331
  93.4 0.1 collective-permute-start.3
  93.5 4.1 %collective-permute-done.4 = f32[17,1536]{1,0:T(8,128)S(1)} collective-permute-done((f32[17,1536]{1,0:T(8,128)S(1)}, f32[17,1536]{1,0:T(8,128)S(1)}, u32[]{:S(2)}, u32[]{:S(2)}) %collective-permute-start.4) | collective-permute-done | bytes 104480 | tf_op jit(solution)/shard_map/ppermute | solution.py:331
  97.6 1.2 %collective-permute-start.5 = (f32[17,1536]{1,0:T(8,128)S(1)}, f32[17,1536]{1,0:T(8,128)S(1)}, u32[]{:S(2)}, u32[]{:S(2)}) collective-permute-start(f32[17,1536]{1,0:T(8,128)S(1)} %select_add_fusion), channel_id=1, source_target_pairs={{0,2},{2,0},{4,6},{6,4},{8,10},{10,8},{12,14},{14,12},{16,18},{18,... | collective-permute-start | bytes 313352 | tf_op jit(solution)/shard_map/ppermute | solution.py:334
  98.9 6.9 %shard_map.67 = f32[17,1536]{1,0:T(8,128)S(1)} custom-call(f32[49,1536]{1,0:T(8,128)S(1)} %collective-permute-done.sibling.source, f32[49,1536]{1,0:T(8,128)S(1)} %constant_dynamic-update-slice_fusion.source.mine, f32[32,1]{1,0:T(8,128)S(1)} %copy.10.inv, f32[17,1536]{1,0:T(8,128)S(1)} %get-tuple-element.535.base), custom_call_target="tpu_custom_call" | custom-call | flops 12079595520 | bytes 706560 | tf_op jit(solution)/shard_map/pallas_call | solution.py:191
  105.8 0.0 collective-permute-done.3
  105.8 0.7 multiply_add_fusion
  (13 shorter events, 0.2 us)
Async XLA Ops:
  0.0 1.0 copy-start
  1.0 3.5 %copy-start.2 = (f32[32]{0:T(128)S(1)}, f32[32]{0:T(128)}, u32[]{:S(2)}) copy-start(f32[32]{0:T(128)} %param.72) | copy-start | bytes 388
  1.0 16.2 %collective-permute-start = (f32[49,1536]{1,0:T(8,128)S(1)}, f32[49,1536]{1,0:T(8,128)S(1)}, u32[]{:S(2)}, u32[]{:S(2)}) collective-permute-start(f32[49,1536]{1,0:T(8,128)S(1)} %constant_dynamic-update-slice_fusion.source.mine), channel_id=1, source_target_pairs={{0,1},{1,0},{2,3},{3,2},{4,5},{5,4},{6,7},{7,6},{8,9},{9,8},{10,11... | collective-permute-start | bytes 903176 | tf_op jit(solution)/shard_map/ppermute | solution.py:312
  3.2 11.4 %collective-permute-start.1 = (f32[49,1536]{1,0:T(8,128)S(1)}, f32[49,1536]{1,0:T(8,128)S(1)}, u32[]{:S(2)}, u32[]{:S(2)}) collective-permute-start(f32[49,1536]{1,0:T(8,128)S(1)} %constant_dynamic-update-slice_fusion.source.mine), channel_id=1, source_target_pairs={{0,2},{2,0},{4,6},{6,4},{8,10},{10,8},{12,14},{14,12},{16,18},{18,... | collective-permute-start | bytes 903176 | tf_op jit(solution)/shard_map/ppermute | solution.py:311
  11.5 0.7 copy-start.1
  14.7 11.8 %collective-permute-start.2 = (f32[49,1536]{1,0:T(8,128)S(1)}, f32[49,1536]{1,0:T(8,128)S(1)}, u32[]{:S(2)}, u32[]{:S(2)}) collective-permute-start(f32[49,1536]{1,0:T(8,128)S(1)} %broadcast_select_fusion), channel_id=1, source_target_pairs={{0,4},{2,6},{4,0},{6,2},{8,12},{10,14},{12,8},{14,10},{16,20},{18,... | collective-permute-start | bytes 903176 | tf_op jit(solution)/shard_map/ppermute | solution.py:316
  90.5 7.1 %collective-permute-start.4 = (f32[17,1536]{1,0:T(8,128)S(1)}, f32[17,1536]{1,0:T(8,128)S(1)}, u32[]{:S(2)}, u32[]{:S(2)}) collective-permute-start(f32[17,1536]{1,0:T(8,128)S(1)} %broadcast_select_fusion.2), channel_id=1, source_target_pairs={{0,4},{2,6},{4,0},{6,2},{8,12},{10,14},{12,8},{14,10},{16,20},{18,... | collective-permute-start | bytes 313352 | tf_op jit(solution)/shard_map/ppermute | solution.py:331
  93.4 12.4 %collective-permute-start.3 = (f32[17,1536]{1,0:T(8,128)S(1)}, f32[17,1536]{1,0:T(8,128)S(1)}, u32[]{:S(2)}, u32[]{:S(2)}) collective-permute-start(f32[17,1536]{1,0:T(8,128)S(1)} %get-tuple-element.536), channel_id=1, source_target_pairs={{0,1},{1,0},{2,3},{3,2},{4,5},{5,4},{6,7},{7,6},{8,9},{9,8},{10,11... | collective-permute-start | bytes 313352 | tf_op jit(solution)/shard_map/ppermute | solution.py:329
  97.6 8.2 %collective-permute-start.5 = (f32[17,1536]{1,0:T(8,128)S(1)}, f32[17,1536]{1,0:T(8,128)S(1)}, u32[]{:S(2)}, u32[]{:S(2)}) collective-permute-start(f32[17,1536]{1,0:T(8,128)S(1)} %select_add_fusion), channel_id=1, source_target_pairs={{0,2},{2,0},{4,6},{6,4},{8,10},{10,8},{12,14},{14,12},{16,18},{18,... | collective-permute-start | bytes 313352 | tf_op jit(solution)/shard_map/ppermute | solution.py:334
where the time goes:
time: 107 us
  Pallas kernels  86.7 us (81%)
  starting transfers between devices  8.75 us (8%)
  waiting for transfers between devices  4.16 us (4%)
  between operations  3.31 us (3%)
  local copies, waits for them, and re-layouts  2.44 us (2%)
    pallas_call x2, Pallas kernels, exchange(): pl.pallas_call(functools.partial(exchange_body, route=route), out_shape=(...  45.2 us
    pallas_call x4, Pallas kernels, tile_call(): pl.pallas_call(body, out_shape=(jax.ShapeDtypeStruct((17, n), F32),) * ou...  41.5 us
    ppermute x1, waiting for transfers between devices, local(): from_across = lax.ppermute(jnp.where(lent_far, returned, 0.0), 'blk', apart)  4.14 us
    ppermute x1, starting transfers between devices, local(): across = lax.ppermute(lent, 'blk', apart)  2.45 us
    ppermute x1, starting transfers between devices, local(): sibling = lax.ppermute(mine, 'half', swap)  2.21 us
  transfers between devices with their start and end apart: 6, of which 1 were waited for; matrix products, arithmetic and copies ran while one was open for 1% of the time, Pallas kernels for 22%

commit v1 on v0

v1 whole, which is shorter than its diff:
```python
import functools
import math

import jax
import jax.numpy as jnp
import numpy as np
from jax import lax
from jax.experimental import pallas as pl
from jax.experimental.pallas import tpu as pltpu
from jax.sharding import PartitionSpec as P

F32 = jnp.float32
BF16 = jnp.bfloat16
LOW = jnp.float8_e5m2
LOG2E = math.log2(math.e)
ALPHA = 1.5 * LOG2E
BETA = 0.75 * LOG2E * LOG2E
FACTOR = math.exp(1.5) / (3.0 * LOG2E * LOG2E)
STRETCH = math.sqrt(5.0) * LOG2E
TINY = 1e-30
DEPTH = 256
COLUMNS = 256
ROWS = 768


def pieces(x, count):
    out = []
    for _ in range(count):
        part = x.astype(BF16).astype(F32)
        out.append(part)
        x = x - part
    return out


def features(points, inv):
    x = points * inv
    norm = jnp.sum(x * x, axis=0, keepdims=True)
    return pieces(x, 3), pieces(norm, 3)


def row_side(points, inv):
    (h, m, l), norm = features(points, inv)
    one = jnp.ones_like(norm[0])
    tail = jnp.concatenate(norm + [one, one, one], axis=0)
    rest = jnp.zeros((DEPTH - 198, points.shape[1]), F32)
    return jnp.concatenate([-2.0 * p for p in (h, h, m, h, l, m)] + [tail, rest], axis=0).astype(BF16)


def column_side(points, inv):
    (h, m, l), norm = features(points, inv)
    one = jnp.ones_like(norm[0])
    tail = jnp.concatenate([one, one, one] + norm, axis=0)
    rest = jnp.zeros((DEPTH - 198, points.shape[1]), F32)
    return jnp.concatenate([h, m, h, l, h, m, tail, rest], axis=0).astype(BF16)


def vector_side(vectors):
    pad = jnp.zeros((7, vectors.shape[1]), F32)
    hi, lo = pieces(vectors, 2)
    wide = jnp.concatenate([hi, pad, lo, pad], axis=0).astype(BF16)
    first = vectors.astype(LOW).astype(F32)
    second = vectors - first
    fill = jnp.zeros((16, vectors.shape[1]), F32)
    low = jnp.concatenate([first, pad, second, pad, fill], axis=0).astype(LOW)
    return wide, low


def kernel_values(squared):
    q = jnp.maximum(squared, TINY)
    h = -ALPHA - q * lax.rsqrt(q)
    values = (h * h + BETA) * jnp.exp2(h)
    hi = values.astype(BF16)
    return hi, (values - hi.astype(F32)).astype(LOW)


def dot(a, b):
    return jnp.dot(a, b, preferred_element_type=F32)


def dot_t(a, b):
    return lax.dot_general(a, b, (((1,), (1,)), ((), ())), preferred_element_type=F32)


def folded(wide, low):
    return wide[0:24] + wide[24:48] + low[0:24] + low[24:48]


def column_step(i):
    return pl.ds(pl.multiple_of(i * COLUMNS, COLUMNS), COLUMNS)


def by_columns(n, step):
    def run(i, carry):
        step(pl.ds(pl.multiple_of(i * COLUMNS, COLUMNS), COLUMNS))
        return carry

    lax.fori_loop(0, n // COLUMNS, run, 0)


def one_way_body(source, mine, inv, base, *refs):
    before, (out, rows, vec, low, cols) = refs[:-5], refs[-5:]
    n = mine.shape[1]
    at = rows.shape[0] - 1

    def prepare(c):
        if before:
            rows[0, c, :] = before[0][0, c, :]
            vec[0, :, c], low[0, :, c] = before[1][0, :, c], before[2][0, :, c]
        rows[at, c, :] = row_side(source[0:32, c], inv[...]).T
        vec[at, :, c], low[at, :, c] = vector_side(source[32:49, c])
        cols[:, c] = column_side(mine[0:32, c], inv[...])

    def step(c):
        hi, lo = kernel_values(dot(rows[at], cols[:, c]))
        out[:, c] = base[:, c] + folded(dot(vec[at], hi), dot(low[at], lo))[0:17]

    by_columns(n, prepare)
    by_columns(n, step)


def estimate(n, passes):
    return pl.CostEstimate(flops=2 * n * n * 256 * passes, bytes_accessed=4 * 115 * n, transcendentals=2 * n * n)


def one_way(source, mine, inv, base, before=()):
    n = mine.shape[1]
    halves = 2 if before else 1
    return pl.pallas_call(
        one_way_body,
        out_shape=(
            jax.ShapeDtypeStruct((17, n), F32),
            jax.ShapeDtypeStruct((halves, n, DEPTH), BF16),
            jax.ShapeDtypeStruct((halves, 48, n), BF16),
            jax.ShapeDtypeStruct((halves, 64, n), LOW),
        ),
        scratch_shapes=[pltpu.VMEM((DEPTH, n), BF16)],
        cost_estimate=estimate(n, 10),
        compiler_params=pltpu.CompilerParams(vmem_limit_bytes=48 << 20),
    )(source, mine, inv, base, *before)


AXES = ("blk", "half")
MESH = pl.DeviceIdType.MESH


def rounds_body(
    sent, beside, inv, base, rows, vec_r, low_r, own, for_sibling, for_beside, returned, *scratch, route
):
    land, cols, vec_c, low_c, acc, acc_low, par, back, sems, back_sems = scratch
    n = beside.shape[1]
    parts = n // ROWS
    steps = n // COLUMNS
    mask, last, kind = route
    block, half = lax.axis_index("blk"), lax.axis_index("half")
    core = lax.rem(block, 2)
    bits = {k: lax.rem(lax.div(block, 1 << k), 2) for k in range(last.bit_length()) if (mask | kind) >> k & 1}
    one = block + mask - sum(bits[k] * (2 << k) for k in bits if mask >> k & 1)
    two = last - block
    change = lax.rem(sum(bits[k] for k in bits if kind >> k & 1), 2) * (two - one)
    to, sender = (one + change, half), (two - change, half)

    barrier = pltpu.get_barrier_semaphore()
    for device in (to, sender):
        pl.semaphore_signal(barrier, inc=1, device_id=device, device_id_type=MESH)
    pl.semaphore_wait(barrier, 2)
    fetch = pltpu.make_async_remote_copy(
        src_ref=sent,
        dst_ref=land.at[1],
        send_sem=sems.at[0],
        recv_sem=sems.at[1],
        device_id=to,
        device_id_type=MESH,
    )
    fetch.start()

    def give(i):
        c = pl.ds(pl.multiple_of(i * COLUMNS, COLUMNS), COLUMNS)
        return pltpu.make_async_remote_copy(
            src_ref=par.at[1, :, c],
            dst_ref=back.at[:, c],
            send_sem=back_sems.at[0, i],
            recv_sem=back_sems.at[1, i],
            device_id=sender,
            device_id_type=MESH,
        )

    def clear(c):
        land[0, :, c] = beside[:, c]
        acc[:, :, c] = jnp.zeros((2, 48, COLUMNS), F32)
        acc_low[:, :, c] = jnp.zeros((2, 64, COLUMNS), F32)
        par[:, :, c] = jnp.zeros((2, 24, COLUMNS), F32)

    by_columns(n, clear)

    first = steps * parts

    def tile(i, carry):
        late = lax.div(lax.div(i, first) + 1, 2)
        left = i - late * first
        visits = (1 + late) * parts
        at = lax.div(left, visits)
        visit = lax.rem(left, visits)
        row = (1 - late) * core + late * lax.div(visit, parts)
        c = pl.ds(pl.multiple_of(at * COLUMNS, COLUMNS), COLUMNS)
        r = pl.ds(pl.multiple_of(lax.rem(visit, parts) * ROWS, ROWS), ROWS)

        @pl.when(i == first)
        def _():
            fetch.wait()

        @pl.when(visit == 0)
        def _():
            other = land[late, :, c]
            cols[...] = column_side(other[0:32, :], inv[...])
            vec_c[...], low_c[...] = vector_side(other[32:49, :])

        hi, lo = kernel_values(dot(rows[row, r, :], cols[...]))
        par[late, :, c] += folded(dot(vec_r[row, :, r], hi), dot(low_r[row, :, r], lo))
        acc[row, :, r] += dot_t(vec_c[...], hi)
        acc_low[row, :, r] += dot_t(low_c[...], lo)

        @pl.when(late * visit == 2 * parts - 1)
        def _():
            give(at).start()

        return carry

    lax.fori_loop(0, 3 * first, tile, 0)

    def total(c):
        own[:, c] = base[:, c] + folded(acc[0, :, c], acc_low[0, :, c])[0:17]
        for_sibling[:, c] = folded(acc[1, :, c], acc_low[1, :, c])[0:17]
        for_beside[:, c] = par[0, 0:17, c]

    def finish(i, carry):
        give(i).wait()
        c = pl.ds(pl.multiple_of(i * COLUMNS, COLUMNS), COLUMNS)
        returned[:, c] = back[0:17, c]
        return carry

    by_columns(n, total)
    lax.fori_loop(0, steps, finish, 0)


def rounds(sent, beside, inv, base, rows, vec, low, route, number):
    n = beside.shape[1]
    steps = n // COLUMNS
    whole = pl.BlockSpec(memory_space=pltpu.VMEM)
    return pl.pallas_call(
        functools.partial(rounds_body, route=route),
        out_shape=(jax.ShapeDtypeStruct((17, n), F32),) * 4,
        in_specs=[whole] * 7,
        out_specs=(whole,) * 4,
        scratch_shapes=[
            pltpu.VMEM((2, 49, n), F32),
            pltpu.VMEM((DEPTH, COLUMNS), BF16),
            pltpu.VMEM((48, COLUMNS), BF16),
            pltpu.VMEM((64, COLUMNS), LOW),
            pltpu.VMEM((2, 48, n), F32),
            pltpu.VMEM((2, 64, n), F32),
            pltpu.VMEM((2, 24, n), F32),
            pltpu.VMEM((24, n), F32),
            pltpu.SemaphoreType.DMA((2,)),
            pltpu.SemaphoreType.DMA((2, steps)),
        ],
        cost_estimate=estimate(n, 60),
        compiler_params=pltpu.CompilerParams(
            collective_id=number, has_side_effects=True, vmem_limit_bytes=48 << 20
        ),
    )(sent, beside, inv, base, rows, vec, low)


def hops(size, start, flip):
    away = ((start ^ flip) - start) % size
    ways = []
    if away and 2 * away <= size:
        ways.append((0, [(start + k) % size for k in range(away)], 0.5 if 2 * away == size else 1.0))
    if away and 2 * away >= size:
        ways.append((1, [(start - k) % size for k in range(size - away)], 0.5 if 2 * away == size else 1.0))
    return ways


RINGS = ((4, 5, 2), (8, 2, 3), (2, 1, 1))


def loads_of(mask, blocks):
    out = np.zeros((blocks, 3, 2, blocks), np.float32)
    for block in range(blocks):
        at = block
        for axis, (size, low, bits) in enumerate(RINGS):
            field = ((1 << bits) - 1) << low
            for way, places, share in hops(size, (at & field) >> low, (mask & field) >> low):
                for place in places:
                    out[block, axis, way, ((at & ~field) | (place << low)) & ~1] += share
            at = (at & ~field) | ((block ^ mask) & field)
    return out.reshape(blocks, -1)


def parity(x):
    return bin(x).count("1") & 1


def mate_routes(blocks):
    last = blocks - 1
    masks = range(4, blocks, 4)
    loads = {m: loads_of(m, blocks) for m in [*masks, last]}
    kinds = np.array([[parity(w & b) for b in range(blocks)] for w in range(blocks)], np.float32)
    routes = [(2, last, 2)]
    for mask in masks:
        worst = (kinds @ (loads[last] - loads[mask]) + loads[mask].sum(0)).max(1)
        fits = [w for w in range(0, blocks, 4) if parity(w & mask) and parity(w & last)]
        best = min(fits, key=lambda w: (round(float(worst[w]), 3), bin(w).count(str(1)), w))
        routes.append((mask, last, best))
    return routes


def local(points, vectors, inv_length, signal_var, noise_var, masks):
    inv = (inv_length * STRETCH)[:, None]
    mine = jnp.concatenate([points, vectors], axis=0)
    blocks = lax.axis_size("blk")
    last = blocks - 1
    middle = masks[0] ^ masks[1] ^ masks[2] ^ 1 ^ last
    which = middle >> 2
    routes = mate_routes(blocks)
    block = lax.axis_index("blk")
    kind = jnp.int32(0)
    for k in range(last.bit_length()):
        having = sum(1 << i for i, r in enumerate(routes) if r[2] >> k & 1)
        kind = kind ^ (np.uint32(having).astype(np.int32) >> which & block >> k & 1)
    lends = kind == 0
    lent_chip = lends & (middle & 1 == 1)
    lent_far = lends & (middle & 2 == 2) & (which > 0)

    chip = [(b, b ^ 1) for b in range(blocks)]
    apart = [(b, b ^ 2) for b in range(blocks)]
    swap = [(0, 1), (1, 0)]
    beside = lax.ppermute(mine, "blk", chip)
    sibling = lax.ppermute(mine, "half", swap)
    own, *before = one_way(mine, mine, inv, jnp.zeros_like(vectors))
    beside, own = lax.optimization_barrier((beside, own))
    lent = jnp.where(lent_chip, beside, mine)
    across = lax.ppermute(lent, "blk", apart)
    own, *rows = one_way(sibling, mine, inv, own, before)
    across, own = lax.optimization_barrier((across, own))
    sent = jnp.where(lent_far, across, lent)
    ways = [functools.partial(rounds, route=r, number=k) for k, r in enumerate(routes)]
    own, for_sibling, for_beside, returned = lax.switch(which, ways, sent, beside, inv, own, *rows)
    from_sibling = lax.ppermute(for_sibling, "half", swap)
    from_across = lax.ppermute(jnp.where(lent_far, returned, 0.0), "blk", apart)
    kept = jnp.where(lent_far, 0.0, returned) + from_across
    from_beside = lax.ppermute(for_beside + jnp.where(lent_chip, kept, 0.0), "blk", chip)
    sums = own + from_sibling + from_beside + jnp.where(lent_chip, 0.0, kept)
    return (signal_var[0] * FACTOR) * sums + noise_var[0] * vectors


def solution(mesh):
    return jax.shard_map(
        local,
        mesh=mesh,
        in_specs=(P(None, AXES), P(None, AXES), P(), P(), P(), P()),
        out_specs=P(None, AXES),
        check_vma=False,
    )
```

time: 107 us -> 95.7 us (0.89)
  Pallas kernels: 86.7 us -> 70.6 us
  starting transfers between devices: 8.75 us -> 11.1 us
  waiting for transfers between devices: 4.16 us -> 6.01 us
    pallas_call x6 -> x3, Pallas kernels: 86.7 us -> 70.6 us  [the longest x1 56.5 us: rounds(): pl.pallas_call(functools.partial(rounds_body, route=route), out_shape=(ja...]
    ppermute x1, starting transfers between devices: 1.24 us -> 3.94 us  [local(): lax.ppermute(for_beside + jnp.where(lent_chip, kept, 0.0), 'blk', chip)]
    ppermute x1, waiting for transfers between devices: 0.01 us -> 1.68 us  [local(): across = lax.ppermute(lent, 'blk', apart)]
  transfers between devices with their start and end apart: 6 -> 6, of which waited for: 1 -> 2; matrix products, arithmetic and copies ran while one was open for 1% -> 2% of each run, Pallas kernels for 22% -> 15%
where the time goes in v1:
time: 95.7 us; the launch traced here: 95.5 us
  Pallas kernels  70.6 us (74%)
  starting transfers between devices  11.1 us (12%)
  waiting for transfers between devices  6.01 us (6%)
  between operations  3.28 us (3%)
  local copies, waits for them, and re-layouts  2.7 us (3%)
  other arithmetic  1.51 us (2%)
    pallas_call x1, Pallas kernels, rounds(): pl.pallas_call(functools.partial(rounds_body, route=route), out_shape=(ja...  56.5 us
    pallas_call x2, Pallas kernels, one_way(): pl.pallas_call(one_way_body, out_shape=(jax.ShapeDtypeStruct((17, n), F32...  14.1 us
    ppermute x1, waiting for transfers between devices, local(): from_across = lax.ppermute(jnp.where(lent_far, returned, 0.0), 'blk', apart)  4.32 us
    ppermute x1, starting transfers between devices, local(): lax.ppermute(for_beside + jnp.where(lent_chip, kept, 0.0), 'blk', chip)  3.94 us
    ppermute x1, starting transfers between devices, local(): across = lax.ppermute(lent, 'blk', apart)  2.45 us
    ppermute x1, starting transfers between devices, local(): sibling = lax.ppermute(mine, 'half', swap)  2.21 us
  transfers between devices with their start and end apart: 6, of which 2 were waited for; matrix products, arithmetic and copies ran while one was open for 2% of the time, Pallas kernels for 15%

profile of v1, /device:TPU:1, one launch (start us, length us, event | category | flops | bytes accessed | tf_op | source)
XLA Modules:
  0.0 95.5 jit_solution(6653454839900893279)
XLA Ops:
  0.0 0.9 constant_dynamic-update-slice_fusion.1
  0.9 0.9 constant_dynamic-update-slice_fusion.source.mine
  1.9 2.2 %collective-permute-start.2 = (f32[49,1536]{1,0:T(8,128)S(1)}, f32[49,1536]{1,0:T(8,128)S(1)}, u32[]{:S(2)}, u32[]{:S(2)}) collective-permute-start(f32[49,1536]{1,0:T(8,128)S(1)} %constant_dynamic-update-slice_fusion.source.mine), channel_id=1, source_target_pairs={{0,1},{1,0},{2,3},{3,2},{4,5},{5,4},{6,7},{7,6},{8,9},{9,8},{10,11... | collective-permute-start | bytes 903176 | tf_op jit(solution)/shard_map/ppermute | solution.py:338
  4.1 1.2 %collective-permute-start = (f32[49,1536]{1,0:T(8,128)S(1)}, f32[49,1536]{1,0:T(8,128)S(1)}, u32[]{:S(2)}, u32[]{:S(2)}) collective-permute-start(f32[49,1536]{1,0:T(8,128)S(1)} %constant_dynamic-update-slice_fusion.source.mine), channel_id=1, source_target_pairs={{0,2},{2,0},{4,6},{6,4},{8,10},{10,8},{12,14},{14,12},{16,18},{18,... | collective-permute-start | bytes 903176 | tf_op jit(solution)/shard_map/ppermute | solution.py:337
  5.3 0.7 multiply_bitcast_fusion
  6.0 0.1 copy.7.inv
  6.1 0.0 copy-start.1
  6.1 7.0 %shard_map.64 = (f32[17,1536]{1,0:T(8,128)S(1)}, bf16[1,1536,256]{2,1,0:T(8,128)(2,1)S(1)}, bf16[1,48,1536]{2,1,0:T(8,128)(2,1)S(1)}, f8e5m2[1,64,1536]{2,1,0:T(32,128)(4,1)S(1)}) custom-call(f32[49,1536]{1,0:T(8,128)S(1)} %constant_dynamic-update-slice_fusion.source.mine, f32[49,1536]{1,0:T(8,128)S(1)} %constant_dynamic-update-slice_fusion.source.mine, ...), custom_call_target="tpu_custom_call" | custom-call | flops 12079595520 | bytes 706560 | tf_op jit(solution)/shard_map/pallas_call | solution.py:128
  13.0 0.0 copy-done.1
  13.0 0.6 fusion
  15.6 0.0 collective-permute-done
  15.6 0.1 broadcast_select_fusion
  15.6 2.4 %collective-permute-start.1 = (f32[49,1536]{1,0:T(8,128)S(1)}, f32[49,1536]{1,0:T(8,128)S(1)}, u32[]{:S(2)}, u32[]{:S(2)}) collective-permute-start(f32[49,1536]{1,0:T(8,128)S(1)} %broadcast_select_fusion), channel_id=1, source_target_pairs={{0,4},{2,6},{4,0},{6,2},{8,12},{10,14},{12,8},{14,10},{16,20},{18,... | collective-permute-start | bytes 903176 | tf_op jit(solution)/shard_map/ppermute | solution.py:342
  18.1 0.0 collective-permute-done.2.source
  18.1 7.1 %shard_map.65 = (f32[17,1536]{1,0:T(8,128)S(1)}, bf16[2,1536,256]{2,1,0:T(8,128)(2,1)}, bf16[2,48,1536]{2,1,0:T(8,128)(2,1)S(1)}, f8e5m2[2,64,1536]{2,1,0:T(32,128)(4,1)S(1)}) custom-call(f32[49,1536]{1,0:T(8,128)S(1)} %collective-permute-done.2.source, f32[49,1536]{1,0:T(8,128)S(1)} %constant_dynamic-update-slice_fusion.source.mine, f32[32,1]{1,0:T(8,128)S(1)} %copy.7.inv, ...), custom_call_target="tpu_custom_call" | custom-call | flops 12079595520 | bytes 706560 | tf_op jit(solution)/shard_map/pallas_call | solution.py:128
  25.2 1.7 %collective-permute-done.1 = f32[49,1536]{1,0:T(8,128)S(1)} collective-permute-done((f32[49,1536]{1,0:T(8,128)S(1)}, f32[49,1536]{1,0:T(8,128)S(1)}, u32[]{:S(2)}, u32[]{:S(2)}) %collective-permute-start.1) | collective-permute-done | bytes 301088 | tf_op jit(solution)/shard_map/ppermute | solution.py:342
  26.9 0.0 copy-start
  26.9 56.9 %conditional.1 = ((f32[17,1536]{1,0:T(8,128)S(1)}, f32[17,1536]{1,0:T(8,128)S(1)}, f32[17,1536]{1,0:T(8,128)S(1)}, f32[17,1536]{1,0:T(8,128)S(1)})) conditional(s32[]{:T(128)} %bitcast.1, (f32[49,1536]{1,0:T(8,128)S(1)}, f32[49,1536]{1,0:T(8,128)S(1)}, f32[32,1]{0,1:T(1,128)S(1)}, f32[17,1536]{1,0:T(8,128)S(1)}, ...), branch_computations={%region_0.1_spmd, %region_1.2_spmd, %region_2.3_spmd, %region_3.4_... | conditional | flops 72477573120 | bytes 706824 | solution.py:347
  27.2 0.1 copy.29.inv
  27.3 56.5 %branch_20_fun.1 = (f32[17,1536]{1,0:T(8,128)S(1)}, f32[17,1536]{1,0:T(8,128)S(1)}, f32[17,1536]{1,0:T(8,128)S(1)}, f32[17,1536]{1,0:T(8,128)S(1)}) custom-call(f32[49,1536]{1,0:T(8,128)S(1)} %get-tuple-element.593.sent, f32[49,1536]{1,0:T(8,128)S(1)} %get-tuple-element.594.beside, f32[32,1]{1,0:T(8,128)S(1)} %copy.29.inv, ...), custom_call_target="tpu_custom_call" | custom-call | flops 72477573120 | bytes 706560 | tf_op jit(solution)/shard_map/cond/branch_20_fun/pallas_call | solution.py:249
  83.9 1.3 %collective-permute-start.4 = (f32[17,1536]{1,0:T(8,128)S(1)}, f32[17,1536]{1,0:T(8,128)S(1)}, u32[]{:S(2)}, u32[]{:S(2)}) collective-permute-start(f32[17,1536]{1,0:T(8,128)S(1)} %broadcast_select_fusion.2), channel_id=1, source_target_pairs={{0,4},{2,6},{4,0},{6,2},{8,12},{10,14},{12,8},{14,10},{16,20},{18,... | collective-permute-start | bytes 313352 | tf_op jit(solution)/shard_map/ppermute | solution.py:349
  85.1 4.3 %collective-permute-done.4 = f32[17,1536]{1,0:T(8,128)S(1)} collective-permute-done((f32[17,1536]{1,0:T(8,128)S(1)}, f32[17,1536]{1,0:T(8,128)S(1)}, u32[]{:S(2)}, u32[]{:S(2)}) %collective-permute-start.4) | collective-permute-done | bytes 104480 | tf_op jit(solution)/shard_map/ppermute | solution.py:349
  89.5 3.9 %collective-permute-start.5 = (f32[17,1536]{1,0:T(8,128)S(1)}, f32[17,1536]{1,0:T(8,128)S(1)}, u32[]{:S(2)}, u32[]{:S(2)}) collective-permute-start(f32[17,1536]{1,0:T(8,128)S(1)} %select_add_fusion), channel_id=1, source_target_pairs={{0,2},{2,0},{4,6},{6,4},{8,10},{10,8},{12,14},{14,12},{16,18},{18,... | collective-permute-start | bytes 313352 | tf_op jit(solution)/shard_map/ppermute | solution.py:351
  94.7 0.7 multiply_add_fusion
  (8 shorter events, 0.1 us)
Async XLA Ops:
  1.9 16.2 %collective-permute-start.2 = (f32[49,1536]{1,0:T(8,128)S(1)}, f32[49,1536]{1,0:T(8,128)S(1)}, u32[]{:S(2)}, u32[]{:S(2)}) collective-permute-start(f32[49,1536]{1,0:T(8,128)S(1)} %constant_dynamic-update-slice_fusion.source.mine), channel_id=1, source_target_pairs={{0,1},{1,0},{2,3},{3,2},{4,5},{5,4},{6,7},{7,6},{8,9},{9,8},{10,11... | collective-permute-start | bytes 903176 | tf_op jit(solution)/shard_map/ppermute | solution.py:338
  4.1 11.5 %collective-permute-start = (f32[49,1536]{1,0:T(8,128)S(1)}, f32[49,1536]{1,0:T(8,128)S(1)}, u32[]{:S(2)}, u32[]{:S(2)}) collective-permute-start(f32[49,1536]{1,0:T(8,128)S(1)} %constant_dynamic-update-slice_fusion.source.mine), channel_id=1, source_target_pairs={{0,2},{2,0},{4,6},{6,4},{8,10},{10,8},{12,14},{14,12},{16,18},{18,... | collective-permute-start | bytes 903176 | tf_op jit(solution)/shard_map/ppermute | solution.py:337
  6.1 7.0 %copy-start.1 = (s32[3]{0:T(128)S(1)}, s32[3]{0:T(128)}, u32[]{:S(2)}) copy-start(s32[3]{0:T(128)} %param.43) | copy-start | bytes 40
  15.6 11.3 %collective-permute-start.1 = (f32[49,1536]{1,0:T(8,128)S(1)}, f32[49,1536]{1,0:T(8,128)S(1)}, u32[]{:S(2)}, u32[]{:S(2)}) collective-permute-start(f32[49,1536]{1,0:T(8,128)S(1)} %broadcast_select_fusion), channel_id=1, source_target_pairs={{0,4},{2,6},{4,0},{6,2},{8,12},{10,14},{12,8},{14,10},{16,20},{18,... | collective-permute-start | bytes 903176 | tf_op jit(solution)/shard_map/ppermute | solution.py:342
  26.9 67.8 %copy-start = (f32[17,1536]{1,0:T(8,128)S(1)}, f32[17,1536]{1,0:T(8,128)}, u32[]{:S(2)}) copy-start(f32[17,1536]{1,0:T(8,128)} %param.39) | copy-start | bytes 313348
  83.9 5.6 %collective-permute-start.4 = (f32[17,1536]{1,0:T(8,128)S(1)}, f32[17,1536]{1,0:T(8,128)S(1)}, u32[]{:S(2)}, u32[]{:S(2)}) collective-permute-start(f32[17,1536]{1,0:T(8,128)S(1)} %broadcast_select_fusion.2), channel_id=1, source_target_pairs={{0,4},{2,6},{4,0},{6,2},{8,12},{10,14},{12,8},{14,10},{16,20},{18,... | collective-permute-start | bytes 313352 | tf_op jit(solution)/shard_map/ppermute | solution.py:349
  85.1 9.6 %collective-permute-start.3 = (f32[17,1536]{1,0:T(8,128)S(1)}, f32[17,1536]{1,0:T(8,128)S(1)}, u32[]{:S(2)}, u32[]{:S(2)}) collective-permute-start(f32[17,1536]{1,0:T(8,128)S(1)} %get-tuple-element.706), channel_id=1, source_target_pairs={{0,1},{1,0},{2,3},{3,2},{4,5},{5,4},{6,7},{7,6},{8,9},{9,8},{10,11... | collective-permute-start | bytes 313352 | tf_op jit(solution)/shard_map/ppermute | solution.py:348
  89.5 5.2 %collective-permute-start.5 = (f32[17,1536]{1,0:T(8,128)S(1)}, f32[17,1536]{1,0:T(8,128)S(1)}, u32[]{:S(2)}, u32[]{:S(2)}) collective-permute-start(f32[17,1536]{1,0:T(8,128)S(1)} %select_add_fusion), channel_id=1, source_target_pairs={{0,2},{2,0},{4,6},{6,4},{8,10},{10,8},{12,14},{14,12},{16,18},{18,... | collective-permute-start | bytes 313352 | tf_op jit(solution)/shard_map/ppermute | solution.py:351

commit v2 on v1

--- a/solution.py
+++ b/solution.py
@@ -20,7 +20,8 @@
 TINY = 1e-30
 DEPTH = 256
 COLUMNS = 256
-ROWS = 768
+ROWS = 512
+FAR = 1e30
 
 
 def pieces(x, count):
@@ -89,6 +90,10 @@
     return pl.ds(pl.multiple_of(i * COLUMNS, COLUMNS), COLUMNS)
 
 
+def column_step(i):
+    return pl.ds(pl.multiple_of(i * COLUMNS, COLUMNS), COLUMNS)
+
+
 def by_columns(n, step):
     def run(i, carry):
         step(pl.ds(pl.multiple_of(i * COLUMNS, COLUMNS), COLUMNS))
@@ -98,7 +103,7 @@
 
 
 def one_way_body(source, mine, inv, base, *refs):
-    before, (out, rows, vec, low, cols) = refs[:-5], refs[-5:]
+    before, (out, rows, vec, low, cols, far, high, rest) = refs[:-8], refs[-8:]
     n = mine.shape[1]
     at = rows.shape[0] - 1
 
@@ -110,12 +115,20 @@
         vec[at, :, c], low[at, :, c] = vector_side(source[32:49, c])
         cols[:, c] = column_side(mine[0:32, c], inv[...])
 
-    def step(c):
-        hi, lo = kernel_values(dot(rows[at], cols[:, c]))
-        out[:, c] = base[:, c] + folded(dot(vec[at], hi), dot(low[at], lo))[0:17]
+    far[...] = jnp.full(far.shape, FAR, F32)
+    high[...] = jnp.zeros_like(high)
+    rest[...] = jnp.zeros_like(rest)
+    chunks = n // COLUMNS
+
+    def step(i, carry):
+        done = column_step(jnp.maximum(i - 2, 0))
+        out[:, done] = base[:, done] + folded(dot(vec[at], high[...]), dot(low[at], rest[...]))[0:17]
+        high[...], rest[...] = kernel_values(far[...])
+        far[...] = dot(rows[at], cols[:, column_step(jnp.minimum(i, chunks - 1))])
+        return carry
 
     by_columns(n, prepare)
-    by_columns(n, step)
+    lax.fori_loop(0, chunks + 2, step, 0)
 
 
 def estimate(n, passes):
@@ -133,7 +146,12 @@
             jax.ShapeDtypeStruct((halves, 48, n), BF16),
             jax.ShapeDtypeStruct((halves, 64, n), LOW),
         ),
-        scratch_shapes=[pltpu.VMEM((DEPTH, n), BF16)],
+        scratch_shapes=[
+            pltpu.VMEM((DEPTH, n), BF16),
+            pltpu.VMEM((n, COLUMNS), F32),
+            pltpu.VMEM((n, COLUMNS), BF16),
+            pltpu.VMEM((n, COLUMNS), LOW),
+        ],
         cost_estimate=estimate(n, 10),
         compiler_params=pltpu.CompilerParams(vmem_limit_bytes=48 << 20),
     )(source, mine, inv, base, *before)
@@ -146,7 +164,7 @@
 def rounds_body(
     sent, beside, inv, base, rows, vec_r, low_r, own, for_sibling, for_beside, returned, *scratch, route
 ):
-    land, cols, vec_c, low_c, acc, acc_low, par, back, sems, back_sems = scratch
+    land, cols, vec_c, low_c, acc, acc_low, par, back, far, high, rest, sems, back_sems = scratch
     n = beside.shape[1]
     parts = n // ROWS
     steps = n // COLUMNS
@@ -193,16 +211,25 @@
     by_columns(n, clear)
 
     first = steps * parts
-
-    def tile(i, carry):
+    tiles = 3 * first
+
+    def place(i):
         late = lax.div(lax.div(i, first) + 1, 2)
         left = i - late * first
         visits = (1 + late) * parts
-        at = lax.div(left, visits)
         visit = lax.rem(left, visits)
         row = (1 - late) * core + late * lax.div(visit, parts)
-        c = pl.ds(pl.multiple_of(at * COLUMNS, COLUMNS), COLUMNS)
         r = pl.ds(pl.multiple_of(lax.rem(visit, parts) * ROWS, ROWS), ROWS)
+        return late, visit, row, r, lax.div(left, visits)
+
+    far[...] = jnp.full(far.shape, FAR, F32)
+    high[...] = jnp.zeros_like(high)
+    rest[...] = jnp.zeros_like(rest)
+
+    def tile(i, carry):
+        late, visit, row, r, at = place(i - lax.div(i, tiles) * (i - tiles + 1))
+        late_d, visit_d, row_d, r_d, at_d = place((i - 2) * lax.div(i + tiles, tiles + 2))
+        c, c_d = column_step(at), column_step(at_d)
 
         @pl.when(i == first)
         def _():
@@ -212,20 +239,22 @@
         def _():
             other = land[late, :, c]
             cols[...] = column_side(other[0:32, :], inv[...])
-            vec_c[...], low_c[...] = vector_side(other[32:49, :])
-
-        hi, lo = kernel_values(dot(rows[row, r, :], cols[...]))
-        par[late, :, c] += folded(dot(vec_r[row, :, r], hi), dot(low_r[row, :, r], lo))
-        acc[row, :, r] += dot_t(vec_c[...], hi)
-        acc_low[row, :, r] += dot_t(low_c[...], lo)
-
-        @pl.when(late * visit == 2 * parts - 1)
+            vec_c[late, :, c], low_c[late, :, c] = vector_side(other[32:49, :])
+
+        hi, lo = high[...], rest[...]
+        par[late_d, :, c_d] += folded(dot(vec_r[row_d, :, r_d], hi), dot(low_r[row_d, :, r_d], lo))
+        acc[row_d, :, r_d] += dot_t(vec_c[late_d, :, c_d], hi)
+        acc_low[row_d, :, r_d] += dot_t(low_c[late_d, :, c_d], lo)
+        high[...], rest[...] = kernel_values(far[...])
+        far[...] = dot(rows[row, r, :], cols[...])
+
+        @pl.when(late_d * visit_d == 2 * parts - 1)
         def _():
-            give(at).start()
+            give(at_d).start()
 
         return carry
 
-    lax.fori_loop(0, 3 * first, tile, 0)
+    lax.fori_loop(0, tiles + 2, tile, 0)
 
     def total(c):
         own[:, c] = base[:, c] + folded(acc[0, :, c], acc_low[0, :, c])[0:17]
@@ -254,12 +283,15 @@
         scratch_shapes=[
             pltpu.VMEM((2, 49, n), F32),
             pltpu.VMEM((DEPTH, COLUMNS), BF16),
-            pltpu.VMEM((48, COLUMNS), BF16),
-            pltpu.VMEM((64, COLUMNS), LOW),
+            pltpu.VMEM((2, 48, n), BF16),
+            pltpu.VMEM((2, 64, n), LOW),
             pltpu.VMEM((2, 48, n), F32),
             pltpu.VMEM((2, 64, n), F32),
             pltpu.VMEM((2, 24, n), F32),
             pltpu.VMEM((24, n), F32),
+            pltpu.VMEM((ROWS, COLUMNS), F32),
+            pltpu.VMEM((ROWS, COLUMNS), BF16),
+            pltpu.VMEM((ROWS, COLUMNS), LOW),
             pltpu.SemaphoreType.DMA((2,)),
             pltpu.SemaphoreType.DMA((2, steps)),
         ],

time: 95.7 us -> 88.1 us (0.921)
  the two profiles are of different devices: /device:TPU:1 before, /device:TPU:33 now
where the time goes in v2:
time: 88.1 us; the launch traced here: 88 us
  Pallas kernels  66.8 us (76%)
  starting transfers between devices  6.93 us (8%)
  waiting for transfers between devices  6.47 us (7%)
  between operations  3.29 us (4%)
  local copies, waits for them, and re-layouts  2.68 us (3%)
  other arithmetic  1.51 us (2%)
    pallas_call x1, Pallas kernels, rounds(): pl.pallas_call(functools.partial(rounds_body, route=route), out_shape=(ja...  49.8 us
    pallas_call x2, Pallas kernels, one_way(): pl.pallas_call(one_way_body, out_shape=(jax.ShapeDtypeStruct((17, n), F32...  17 us
    ppermute x1, waiting for transfers between devices, local(): from_across = lax.ppermute(jnp.where(lent_far, returned, 0.0), 'blk', apart)  6.45 us
    ppermute x1, starting transfers between devices, local(): across = lax.ppermute(lent, 'blk', apart)  2.71 us
  transfers between devices with their start and end apart: 6, of which 1 were waited for; matrix products, arithmetic and copies ran while one was open for 2% of the time, Pallas kernels for 19%

profile of v2, /device:TPU:33, one launch (start us, length us, event | category | flops | bytes accessed | tf_op | source)
XLA Modules:
  0.0 88.0 jit_solution(17858780841829564809)
XLA Ops:
  0.0 0.9 %constant_dynamic-update-slice_fusion.1 = f32[49,1536]{1,0:T(8,128)S(1)} fusion(f32[32,1536]{1,0:T(8,128)} %param.38), kind=kLoop, calls=%fused_computation.7 | loop fusion | bytes 393216
  0.9 0.9 %constant_dynamic-update-slice_fusion.source.mine = f32[49,1536]{1,0:T(8,128)S(1)} fusion(f32[49,1536]{1,0:T(8,128)S(1)} %constant_dynamic-update-slice_fusion.1, f32[17,1536]{1,0:T(8,128)} %param.39), kind=kLoop, calls=%fused_computation.6 | loop fusion | bytes 251904 | tf_op jit(solution)/shard_map/concatenate | solution.py:351
  1.9 1.4 %collective-permute-start.2 = (f32[49,1536]{1,0:T(8,128)S(1)}, f32[49,1536]{1,0:T(8,128)S(1)}, u32[]{:S(2)}, u32[]{:S(2)}) collective-permute-start(f32[49,1536]{1,0:T(8,128)S(1)} %constant_dynamic-update-slice_fusion.source.mine), channel_id=1, source_target_pairs={{0,1},{1,0},{2,3},{3,2},{4,5},{5,4},{6,7},{7,6},{8,9},{9,8},{10,11... | collective-permute-start | bytes 903176 | tf_op jit(solution)/shard_map/ppermute | solution.py:370
  3.3 1.0 %collective-permute-start = (f32[49,1536]{1,0:T(8,128)S(1)}, f32[49,1536]{1,0:T(8,128)S(1)}, u32[]{:S(2)}, u32[]{:S(2)}) collective-permute-start(f32[49,1536]{1,0:T(8,128)S(1)} %constant_dynamic-update-slice_fusion.source.mine), channel_id=1, source_target_pairs={{0,2},{2,0},{4,6},{6,4},{8,10},{10,8},{12,14},{14,12},{16,18},{18,... | collective-permute-start | bytes 903176 | tf_op jit(solution)/shard_map/ppermute | solution.py:369
  4.2 0.7 multiply_bitcast_fusion
  4.9 0.1 copy.7.inv
  5.0 0.0 copy-start.1
  5.0 8.3 %shard_map.64 = (f32[17,1536]{1,0:T(8,128)S(1)}, bf16[1,1536,256]{2,1,0:T(8,128)(2,1)S(1)}, bf16[1,48,1536]{2,1,0:T(8,128)(2,1)S(1)}, f8e5m2[1,64,1536]{2,1,0:T(32,128)(4,1)S(1)}) custom-call(f32[49,1536]{1,0:T(8,128)S(1)} %constant_dynamic-update-slice_fusion.source.mine, f32[49,1536]{1,0:T(8,128)S(1)} %constant_dynamic-update-slice_fusion.source.mine, ...), custom_call_target="tpu_custom_call" | custom-call | flops 12079595520 | bytes 706560 | tf_op jit(solution)/shard_map/pallas_call | solution.py:141
  13.3 0.6 fusion
  15.8 0.0 collective-permute-done
  15.8 0.1 broadcast_select_fusion
  15.8 2.7 %collective-permute-start.1 = (f32[49,1536]{1,0:T(8,128)S(1)}, f32[49,1536]{1,0:T(8,128)S(1)}, u32[]{:S(2)}, u32[]{:S(2)}) collective-permute-start(f32[49,1536]{1,0:T(8,128)S(1)} %broadcast_select_fusion), channel_id=1, source_target_pairs={{0,4},{2,6},{4,0},{6,2},{8,12},{10,14},{12,8},{14,10},{16,20},{18,... | collective-permute-start | bytes 903176 | tf_op jit(solution)/shard_map/ppermute | solution.py:374
  18.5 8.7 %shard_map.65 = (f32[17,1536]{1,0:T(8,128)S(1)}, bf16[2,1536,256]{2,1,0:T(8,128)(2,1)}, bf16[2,48,1536]{2,1,0:T(8,128)(2,1)S(1)}, f8e5m2[2,64,1536]{2,1,0:T(32,128)(4,1)S(1)}) custom-call(f32[49,1536]{1,0:T(8,128)S(1)} %collective-permute-done.2.source, f32[49,1536]{1,0:T(8,128)S(1)} %constant_dynamic-update-slice_fusion.source.mine, f32[32,1]{1,0:T(8,128)S(1)} %copy.7.inv, ...), custom_call_target="tpu_custom_call" | custom-call | flops 12079595520 | bytes 706560 | tf_op jit(solution)/shard_map/pallas_call | solution.py:141
  27.2 0.0 collective-permute-done.1
  27.3 0.0 copy-start
  27.3 50.2 %conditional.1 = ((f32[17,1536]{1,0:T(8,128)S(1)}, f32[17,1536]{1,0:T(8,128)S(1)}, f32[17,1536]{1,0:T(8,128)S(1)}, f32[17,1536]{1,0:T(8,128)S(1)})) conditional(s32[]{:T(128)} %bitcast.1, (f32[49,1536]{1,0:T(8,128)S(1)}, f32[49,1536]{1,0:T(8,128)S(1)}, f32[32,1]{0,1:T(1,128)S(1)}, f32[17,1536]{1,0:T(8,128)S(1)}, ...), branch_computations={%region_0.1_spmd, %region_1.2_spmd, %region_2.3_spmd, %region_3.4_... | conditional | flops 72477573120 | bytes 706824 | solution.py:379
  27.3 0.1 copy.10.inv
  27.4 49.8 %branch_1_fun.1 = (f32[17,1536]{1,0:T(8,128)S(1)}, f32[17,1536]{1,0:T(8,128)S(1)}, f32[17,1536]{1,0:T(8,128)S(1)}, f32[17,1536]{1,0:T(8,128)S(1)}) custom-call(f32[49,1536]{1,0:T(8,128)S(1)} %get-tuple-element.460.sent, f32[49,1536]{1,0:T(8,128)S(1)} %get-tuple-element.461.beside, f32[32,1]{1,0:T(8,128)S(1)} %copy.10.inv, ...), custom_call_target="tpu_custom_call" | custom-call | flops 72477573120 | bytes 706560 | tf_op jit(solution)/shard_map/cond/branch_1_fun/pallas_call | solution.py:278
  77.5 0.5 collective-permute-start.4
  78.1 0.1 collective-permute-start.3
  78.1 6.5 %collective-permute-done.4 = f32[17,1536]{1,0:T(8,128)S(1)} collective-permute-done((f32[17,1536]{1,0:T(8,128)S(1)}, f32[17,1536]{1,0:T(8,128)S(1)}, u32[]{:S(2)}, u32[]{:S(2)}) %collective-permute-start.4) | collective-permute-done | bytes 104480 | tf_op jit(solution)/shard_map/ppermute | solution.py:381
  84.6 1.3 %collective-permute-start.5 = (f32[17,1536]{1,0:T(8,128)S(1)}, f32[17,1536]{1,0:T(8,128)S(1)}, u32[]{:S(2)}, u32[]{:S(2)}) collective-permute-start(f32[17,1536]{1,0:T(8,128)S(1)} %select_add_fusion), channel_id=1, source_target_pairs={{0,2},{2,0},{4,6},{6,4},{8,10},{10,8},{12,14},{14,12},{16,18},{18,... | collective-permute-start | bytes 313352 | tf_op jit(solution)/shard_map/ppermute | solution.py:383
  87.2 0.0 collective-permute-done.5
  87.2 0.7 multiply_add_fusion
  (8 shorter events, 0.1 us)
Async XLA Ops:
  1.9 16.7 %collective-permute-start.2 = (f32[49,1536]{1,0:T(8,128)S(1)}, f32[49,1536]{1,0:T(8,128)S(1)}, u32[]{:S(2)}, u32[]{:S(2)}) collective-permute-start(f32[49,1536]{1,0:T(8,128)S(1)} %constant_dynamic-update-slice_fusion.source.mine), channel_id=1, source_target_pairs={{0,1},{1,0},{2,3},{3,2},{4,5},{5,4},{6,7},{7,6},{8,9},{9,8},{10,11... | collective-permute-start | bytes 903176 | tf_op jit(solution)/shard_map/ppermute | solution.py:370
  3.3 12.5 %collective-permute-start = (f32[49,1536]{1,0:T(8,128)S(1)}, f32[49,1536]{1,0:T(8,128)S(1)}, u32[]{:S(2)}, u32[]{:S(2)}) collective-permute-start(f32[49,1536]{1,0:T(8,128)S(1)} %constant_dynamic-update-slice_fusion.source.mine), channel_id=1, source_target_pairs={{0,2},{2,0},{4,6},{6,4},{8,10},{10,8},{12,14},{14,12},{16,18},{18,... | collective-permute-start | bytes 903176 | tf_op jit(solution)/shard_map/ppermute | solution.py:369
  5.0 8.3 %copy-start.1 = (s32[3]{0:T(128)S(1)}, s32[3]{0:T(128)}, u32[]{:S(2)}) copy-start(s32[3]{0:T(128)} %param.43) | copy-start | bytes 40
  15.8 11.4 %collective-permute-start.1 = (f32[49,1536]{1,0:T(8,128)S(1)}, f32[49,1536]{1,0:T(8,128)S(1)}, u32[]{:S(2)}, u32[]{:S(2)}) collective-permute-start(f32[49,1536]{1,0:T(8,128)S(1)} %broadcast_select_fusion), channel_id=1, source_target_pairs={{0,4},{2,6},{4,0},{6,2},{8,12},{10,14},{12,8},{14,10},{16,20},{18,... | collective-permute-start | bytes 903176 | tf_op jit(solution)/shard_map/ppermute | solution.py:374
  27.3 59.9 %copy-start = (f32[17,1536]{1,0:T(8,128)S(1)}, f32[17,1536]{1,0:T(8,128)}, u32[]{:S(2)}) copy-start(f32[17,1536]{1,0:T(8,128)} %param.39) | copy-start | bytes 313348
  77.5 7.1 %collective-permute-start.4 = (f32[17,1536]{1,0:T(8,128)S(1)}, f32[17,1536]{1,0:T(8,128)S(1)}, u32[]{:S(2)}, u32[]{:S(2)}) collective-permute-start(f32[17,1536]{1,0:T(8,128)S(1)} %broadcast_select_fusion.2), channel_id=1, source_target_pairs={{0,4},{2,6},{4,0},{6,2},{8,12},{10,14},{12,8},{14,10},{16,20},{18,... | collective-permute-start | bytes 313352 | tf_op jit(solution)/shard_map/ppermute | solution.py:381
  78.1 9.1 %collective-permute-start.3 = (f32[17,1536]{1,0:T(8,128)S(1)}, f32[17,1536]{1,0:T(8,128)S(1)}, u32[]{:S(2)}, u32[]{:S(2)}) collective-permute-start(f32[17,1536]{1,0:T(8,128)S(1)} %get-tuple-element.706), channel_id=1, source_target_pairs={{0,1},{1,0},{2,3},{3,2},{4,5},{5,4},{6,7},{7,6},{8,9},{9,8},{10,11... | collective-permute-start | bytes 313352 | tf_op jit(solution)/shard_map/ppermute | solution.py:380
  84.6 2.6 %collective-permute-start.5 = (f32[17,1536]{1,0:T(8,128)S(1)}, f32[17,1536]{1,0:T(8,128)S(1)}, u32[]{:S(2)}, u32[]{:S(2)}) collective-permute-start(f32[17,1536]{1,0:T(8,128)S(1)} %select_add_fusion), channel_id=1, source_target_pairs={{0,2},{2,0},{4,6},{6,4},{8,10},{10,8},{12,14},{14,12},{16,18},{18,... | collective-permute-start | bytes 313352 | tf_op jit(solution)/shard_map/ppermute | solution.py:383

commit v3 on v2

--- a/solution.py
+++ b/solution.py
@@ -22,6 +22,7 @@
 COLUMNS = 256
 ROWS = 512
 FAR = 1e30
+GREETED = 8
 
 
 def pieces(x, count):
@@ -102,59 +103,41 @@
     lax.fori_loop(0, n // COLUMNS, run, 0)
 
 
-def one_way_body(source, mine, inv, base, *refs):
-    before, (out, rows, vec, low, cols, far, high, rest) = refs[:-8], refs[-8:]
+def one_way_body(mine, sibling, inv, out, rows, vec, low, cols):
     n = mine.shape[1]
-    at = rows.shape[0] - 1
 
     def prepare(c):
-        if before:
-            rows[0, c, :] = before[0][0, c, :]
-            vec[0, :, c], low[0, :, c] = before[1][0, :, c], before[2][0, :, c]
-        rows[at, c, :] = row_side(source[0:32, c], inv[...]).T
-        vec[at, :, c], low[at, :, c] = vector_side(source[32:49, c])
+        for k, side in enumerate((mine, sibling)):
+            rows[k, c, :] = row_side(side[0:32, c], inv[...]).T
+            vec[k, :, c], low[k, :, c] = vector_side(side[32:49, c])
         cols[:, c] = column_side(mine[0:32, c], inv[...])
 
-    far[...] = jnp.full(far.shape, FAR, F32)
-    high[...] = jnp.zeros_like(high)
-    rest[...] = jnp.zeros_like(rest)
-    chunks = n // COLUMNS
-
-    def step(i, carry):
-        done = column_step(jnp.maximum(i - 2, 0))
-        out[:, done] = base[:, done] + folded(dot(vec[at], high[...]), dot(low[at], rest[...]))[0:17]
-        high[...], rest[...] = kernel_values(far[...])
-        far[...] = dot(rows[at], cols[:, column_step(jnp.minimum(i, chunks - 1))])
-        return carry
+    def step(c):
+        hi, lo = kernel_values(dot(rows[0], cols[:, c]))
+        out[:, c] = folded(dot(vec[0], hi), dot(low[0], lo))[0:17]
 
     by_columns(n, prepare)
-    lax.fori_loop(0, chunks + 2, step, 0)
+    by_columns(n, step)
 
 
 def estimate(n, passes):
     return pl.CostEstimate(flops=2 * n * n * 256 * passes, bytes_accessed=4 * 115 * n, transcendentals=2 * n * n)
 
 
-def one_way(source, mine, inv, base, before=()):
+def one_way(mine, sibling, inv):
     n = mine.shape[1]
-    halves = 2 if before else 1
     return pl.pallas_call(
         one_way_body,
         out_shape=(
             jax.ShapeDtypeStruct((17, n), F32),
-            jax.ShapeDtypeStruct((halves, n, DEPTH), BF16),
-            jax.ShapeDtypeStruct((halves, 48, n), BF16),
-            jax.ShapeDtypeStruct((halves, 64, n), LOW),
+            jax.ShapeDtypeStruct((2, n, DEPTH), BF16),
+            jax.ShapeDtypeStruct((2, 48, n), BF16),
+            jax.ShapeDtypeStruct((2, 64, n), LOW),
         ),
-        scratch_shapes=[
-            pltpu.VMEM((DEPTH, n), BF16),
-            pltpu.VMEM((n, COLUMNS), F32),
-            pltpu.VMEM((n, COLUMNS), BF16),
-            pltpu.VMEM((n, COLUMNS), LOW),
-        ],
+        scratch_shapes=[pltpu.VMEM((DEPTH, n), BF16)],
         cost_estimate=estimate(n, 10),
         compiler_params=pltpu.CompilerParams(vmem_limit_bytes=48 << 20),
-    )(source, mine, inv, base, *before)
+    )(mine, sibling, inv)
 
 
 AXES = ("blk", "half")
@@ -162,7 +145,7 @@
 
 
 def rounds_body(
-    sent, beside, inv, base, rows, vec_r, low_r, own, for_sibling, for_beside, returned, *scratch, route
+    sent, beside, mine, inv, base, rows, vec_r, low_r, own, for_sibling, for_beside, returned, *scratch, route
 ):
     land, cols, vec_c, low_c, acc, acc_low, par, back, far, high, rest, sems, back_sems = scratch
     n = beside.shape[1]
@@ -180,21 +163,19 @@
     barrier = pltpu.get_barrier_semaphore()
     for device in (to, sender):
         pl.semaphore_signal(barrier, inc=1, device_id=device, device_id_type=MESH)
-    pl.semaphore_wait(barrier, 2)
     fetch = pltpu.make_async_remote_copy(
         src_ref=sent,
-        dst_ref=land.at[1],
+        dst_ref=land.at[2],
         send_sem=sems.at[0],
         recv_sem=sems.at[1],
         device_id=to,
         device_id_type=MESH,
     )
-    fetch.start()
 
     def give(i):
         c = pl.ds(pl.multiple_of(i * COLUMNS, COLUMNS), COLUMNS)
         return pltpu.make_async_remote_copy(
-            src_ref=par.at[1, :, c],
+            src_ref=par.at[2, :, c],
             dst_ref=back.at[:, c],
             send_sem=back_sems.at[0, i],
             recv_sem=back_sems.at[1, i],
@@ -204,51 +185,59 @@
 
     def clear(c):
         land[0, :, c] = beside[:, c]
+        land[1, :, c] = mine[:, c]
         acc[:, :, c] = jnp.zeros((2, 48, COLUMNS), F32)
         acc_low[:, :, c] = jnp.zeros((2, 64, COLUMNS), F32)
-        par[:, :, c] = jnp.zeros((2, 24, COLUMNS), F32)
+        par[:, :, c] = jnp.zeros((3, 24, COLUMNS), F32)
 
     by_columns(n, clear)
 
     first = steps * parts
-    tiles = 3 * first
+    tiles = 4 * first
 
     def place(i):
-        late = lax.div(lax.div(i, first) + 1, 2)
-        left = i - late * first
+        part = lax.div(i, first)
+        late = lax.div(part, 2)
+        slot = part - lax.div(part, 3)
+        left = i - slot * first
         visits = (1 + late) * parts
         visit = lax.rem(left, visits)
-        row = (1 - late) * core + late * lax.div(visit, parts)
+        row = (1 - late) * ((1 - slot) * core + slot) + late * lax.div(visit, parts)
         r = pl.ds(pl.multiple_of(lax.rem(visit, parts) * ROWS, ROWS), ROWS)
-        return late, visit, row, r, lax.div(left, visits)
+        return slot, late * visit, visit, row, r, lax.div(left, visits)
 
     far[...] = jnp.full(far.shape, FAR, F32)
     high[...] = jnp.zeros_like(high)
     rest[...] = jnp.zeros_like(rest)
 
     def tile(i, carry):
-        late, visit, row, r, at = place(i - lax.div(i, tiles) * (i - tiles + 1))
-        late_d, visit_d, row_d, r_d, at_d = place((i - 2) * lax.div(i + tiles, tiles + 2))
+        slot, _, visit, row, r, at = place(i - lax.div(i, tiles) * (i - tiles + 1))
+        slot_d, visit_d, _, row_d, r_d, at_d = place((i - 2) * lax.div(i + tiles, tiles + 2))
         c, c_d = column_step(at), column_step(at_d)
 
-        @pl.when(i == first)
+        @pl.when(i == GREETED)
+        def _():
+            pl.semaphore_wait(barrier, 2)
+            fetch.start()
+
+        @pl.when(i == 2 * first)
         def _():
             fetch.wait()
 
         @pl.when(visit == 0)
         def _():
-            other = land[late, :, c]
+            other = land[slot, :, c]
             cols[...] = column_side(other[0:32, :], inv[...])
-            vec_c[late, :, c], low_c[late, :, c] = vector_side(other[32:49, :])
+            vec_c[slot, :, c], low_c[slot, :, c] = vector_side(jnp.where(slot == 1, 0.0, other[32:49, :]))
 
         hi, lo = high[...], rest[...]
-        par[late_d, :, c_d] += folded(dot(vec_r[row_d, :, r_d], hi), dot(low_r[row_d, :, r_d], lo))
-        acc[row_d, :, r_d] += dot_t(vec_c[late_d, :, c_d], hi)
-        acc_low[row_d, :, r_d] += dot_t(low_c[late_d, :, c_d], lo)
+        par[slot_d, :, c_d] += folded(dot(vec_r[row_d, :, r_d], hi), dot(low_r[row_d, :, r_d], lo))
+        acc[row_d, :, r_d] += dot_t(vec_c[slot_d, :, c_d], hi)
+        acc_low[row_d, :, r_d] += dot_t(low_c[slot_d, :, c_d], lo)
         high[...], rest[...] = kernel_values(far[...])
         far[...] = dot(rows[row, r, :], cols[...])
 
-        @pl.when(late_d * visit_d == 2 * parts - 1)
+        @pl.when(visit_d == 2 * parts - 1)
         def _():
             give(at_d).start()
 
@@ -257,7 +246,7 @@
     lax.fori_loop(0, tiles + 2, tile, 0)
 
     def total(c):
-        own[:, c] = base[:, c] + folded(acc[0, :, c], acc_low[0, :, c])[0:17]
+        own[:, c] = base[:, c] + (par[1, :, c] + folded(acc[0, :, c], acc_low[0, :, c]))[0:17]
         for_sibling[:, c] = folded(acc[1, :, c], acc_low[1, :, c])[0:17]
         for_beside[:, c] = par[0, 0:17, c]
 
@@ -271,23 +260,23 @@
     lax.fori_loop(0, steps, finish, 0)
 
 
-def rounds(sent, beside, inv, base, rows, vec, low, route, number):
+def rounds(sent, beside, mine, inv, base, rows, vec, low, route, number):
     n = beside.shape[1]
     steps = n // COLUMNS
     whole = pl.BlockSpec(memory_space=pltpu.VMEM)
     return pl.pallas_call(
         functools.partial(rounds_body, route=route),
         out_shape=(jax.ShapeDtypeStruct((17, n), F32),) * 4,
-        in_specs=[whole] * 7,
+        in_specs=[whole] * 8,
         out_specs=(whole,) * 4,
         scratch_shapes=[
-            pltpu.VMEM((2, 49, n), F32),
+            pltpu.VMEM((3, 49, n), F32),
             pltpu.VMEM((DEPTH, COLUMNS), BF16),
-            pltpu.VMEM((2, 48, n), BF16),
-            pltpu.VMEM((2, 64, n), LOW),
+            pltpu.VMEM((3, 48, n), BF16),
+            pltpu.VMEM((3, 64, n), LOW),
             pltpu.VMEM((2, 48, n), F32),
             pltpu.VMEM((2, 64, n), F32),
-            pltpu.VMEM((2, 24, n), F32),
+            pltpu.VMEM((3, 24, n), F32),
             pltpu.VMEM((24, n), F32),
             pltpu.VMEM((ROWS, COLUMNS), F32),
             pltpu.VMEM((ROWS, COLUMNS), BF16),
@@ -295,11 +284,11 @@
             pltpu.SemaphoreType.DMA((2,)),
             pltpu.SemaphoreType.DMA((2, steps)),
         ],
-        cost_estimate=estimate(n, 60),
+        cost_estimate=estimate(n, 80),
         compiler_params=pltpu.CompilerParams(
             collective_id=number, has_side_effects=True, vmem_limit_bytes=48 << 20
         ),
-    )(sent, beside, inv, base, rows, vec, low)
+    )(sent, beside, mine, inv, base, rows, vec, low)
 
 
 def hops(size, start, flip):
@@ -368,15 +357,14 @@
     swap = [(0, 1), (1, 0)]
     beside = lax.ppermute(mine, "blk", chip)
     sibling = lax.ppermute(mine, "half", swap)
-    own, *before = one_way(mine, mine, inv, jnp.zeros_like(vectors))
-    beside, own = lax.optimization_barrier((beside, own))
     lent = jnp.where(lent_chip, beside, mine)
     across = lax.ppermute(lent, "blk", apart)
-    own, *rows = one_way(sibling, mine, inv, own, before)
+    first, lent, sibling = lax.optimization_barrier((mine, lent, sibling))
+    own, *rows = one_way(first, sibling, inv)
     across, own = lax.optimization_barrier((across, own))
     sent = jnp.where(lent_far, across, lent)
     ways = [functools.partial(rounds, route=r, number=k) for k, r in enumerate(routes)]
-    own, for_sibling, for_beside, returned = lax.switch(which, ways, sent, beside, inv, own, *rows)
+    own, for_sibling, for_beside, returned = lax.switch(which, ways, sent, beside, mine, inv, own, *rows)
     from_sibling = lax.ppermute(for_sibling, "half", swap)
     from_across = lax.ppermute(jnp.where(lent_far, returned, 0.0), "blk", apart)
     kept = jnp.where(lent_far, 0.0, returned) + from_across

time: 88.1 us -> 80.9 us (0.918)
  the two profiles are of different devices: /device:TPU:33 before, /device:TPU:1 now
where the time goes in v3:
time: 80.9 us; the launch traced here: 79.9 us
  Pallas kernels  54 us (67%)
  starting transfers between devices  8.73 us (11%)
  waiting for transfers between devices  8.66 us (11%)
  local copies, waits for them, and re-layouts  3.42 us (4%)
  between operations  3.31 us (4%)
  other arithmetic  1.49 us (2%)
    pallas_call x1, Pallas kernels, rounds(): pl.pallas_call(functools.partial(rounds_body, route=route), out_shape=(ja...  46.1 us
    pallas_call x1, Pallas kernels, one_way(): pl.pallas_call(one_way_body, out_shape=(jax.ShapeDtypeStruct((17, n), F32...  7.91 us
    ppermute x1, waiting for transfers between devices, local(): from_across = lax.ppermute(jnp.where(lent_far, returned, 0.0), 'blk', apart)  5.25 us
    ppermute x1, starting transfers between devices, local(): beside = lax.ppermute(mine, 'blk', chip)  3.33 us
    ppermute x1, waiting for transfers between devices, local(): sibling = lax.ppermute(mine, 'half', swap)  3.22 us
    ppermute x1, starting transfers between devices, local(): across = lax.ppermute(lent, 'blk', apart)  2.28 us
    ppermute x1, starting transfers between devices, local(): from_across = lax.ppermute(jnp.where(lent_far, returned, 0.0), 'blk', apart)  1.78 us
  transfers between devices with their start and end apart: 6, of which 3 were waited for; matrix products, arithmetic and copies ran while one was open for 3% of the time, Pallas kernels for 10%

profile of v3, /device:TPU:1, one launch (start us, length us, event | category | flops | bytes accessed | tf_op | source)
XLA Modules:
  0.0 79.9 jit_solution(14662465121435542405)
XLA Ops:
  0.0 0.9 %constant_dynamic-update-slice_fusion.1 = f32[49,1536]{1,0:T(8,128)S(1)} fusion(f32[32,1536]{1,0:T(8,128)} %param.38), kind=kLoop, calls=%fused_computation.7 | loop fusion | bytes 393216
  0.9 0.9 %constant_dynamic-update-slice_fusion.mine = f32[49,1536]{1,0:T(8,128)S(1)} fusion(f32[49,1536]{1,0:T(8,128)S(1)} %constant_dynamic-update-slice_fusion.1, f32[17,1536]{1,0:T(8,128)} %param.39), kind=kLoop, calls=%fused_computation.6 | loop fusion | bytes 251904 | tf_op jit(solution)/shard_map/concatenate | solution.py:340
  1.9 3.3 %collective-permute-start = (f32[49,1536]{1,0:T(8,128)S(1)}, f32[49,1536]{1,0:T(8,128)S(1)}, u32[]{:S(2)}, u32[]{:S(2)}) collective-permute-start(f32[49,1536]{1,0:T(8,128)S(1)} %constant_dynamic-update-slice_fusion.mine), channel_id=1, source_target_pairs={{0,2},{2,0},{4,6},{6,4},{8,10},{10,8},{12,14},{14,12},{16,18},{18,... | collective-permute-start | bytes 903176 | tf_op jit(solution)/shard_map/ppermute | solution.py:358
  5.2 0.0 collective-permute-start.2
  5.2 1.4 %fusion = (s32[1]{0:T(128)}, s32[1]{0:T(128)}, s32[1]{0:T(128)}) fusion(s32[3]{0:T(128)} %param.43), kind=kLoop, calls=%fused_computation.9 | loop fusion | bytes 24 | tf_op jit(solution)/shard_map/slice | solution.py:343
  8.5 0.7 multiply_bitcast_fusion
  9.2 0.1 copy.7.inv
  9.3 0.0 collective-permute-done
  9.3 2.3 %collective-permute-start.1 = (f32[49,1536]{1,0:T(8,128)S(1)}, f32[49,1536]{1,0:T(8,128)S(1)}, u32[]{:S(2)}, u32[]{:S(2)}) collective-permute-start(f32[49,1536]{1,0:T(8,128)S(1)} %broadcast_select_fusion), channel_id=1, source_target_pairs={{0,4},{2,6},{4,0},{6,2},{8,12},{10,14},{12,8},{14,10},{16,20},{18,... | collective-permute-start | bytes 903176 | tf_op jit(solution)/shard_map/ppermute | solution.py:361
  11.6 3.2 %collective-permute-done.2.sibling = f32[49,1536]{1,0:T(8,128)S(1)} collective-permute-done((f32[49,1536]{1,0:T(8,128)S(1)}, f32[49,1536]{1,0:T(8,128)S(1)}, u32[]{:S(2)}, u32[]{:S(2)}) %collective-permute-start.2) | collective-permute-done | bytes 301088 | tf_op jit(solution)/shard_map/ppermute | solution.py:359
  14.8 7.9 %shard_map.64 = (f32[17,1536]{1,0:T(8,128)}, bf16[2,1536,256]{2,1,0:T(8,128)(2,1)S(1)}, bf16[2,48,1536]{2,1,0:T(8,128)(2,1)}, f8e5m2[2,64,1536]{2,1,0:T(32,128)(4,1)S(1)}) custom-call(f32[49,1536]{1,0:T(8,128)S(1)} %constant_dynamic-update-slice_fusion.mine, f32[49,1536]{1,0:T(8,128)S(1)} %collective-permute-done.2.sibling, f32[32,1]{1,0:T(8,128)S(1)} %copy.7.inv), custom_call_target="tpu_custom_call" | custom-call | flops 12079595520 | bytes 706560 | tf_op jit(solution)/shard_map/pallas_call | solution.py:129
  22.7 0.2 collective-permute-done.1
  23.0 0.0 copy-start
  23.0 46.5 %conditional.1 = ((f32[17,1536]{1,0:T(8,128)S(1)}, f32[17,1536]{1,0:T(8,128)S(1)}, f32[17,1536]{1,0:T(8,128)S(1)}, f32[17,1536]{1,0:T(8,128)S(1)})) conditional(s32[]{:T(128)} %bitcast.1, (f32[49,1536]{1,0:T(8,128)S(1)}, f32[49,1536]{1,0:T(8,128)S(1)}, f32[49,1536]{1,0:T(8,128)S(1)}, f32[32,1]{0,1:T(1,128)S(1)}, ...), branch_computations={%region_0.1_spmd, %region_1.2_spmd, %region_2.3_spmd, %region_3.4_... | conditional | flops 96636764160 | bytes 706824 | solution.py:367
  23.2 0.1 copy.26.inv
  23.3 46.1 %branch_18_fun.1 = (f32[17,1536]{1,0:T(8,128)S(1)}, f32[17,1536]{1,0:T(8,128)S(1)}, f32[17,1536]{1,0:T(8,128)S(1)}, f32[17,1536]{1,0:T(8,128)S(1)}) custom-call(f32[49,1536]{1,0:T(8,128)S(1)} %get-tuple-element.661.sent, f32[49,1536]{1,0:T(8,128)S(1)} %get-tuple-element.662.beside, f32[49,1536]{1,0:T(8,128)S(1)} %get-tuple-element.663.mine, ...), custom_call_target="tpu_custom_call" | custom-call | flops 96636764160 | bytes 706560 | tf_op jit(solution)/shard_map/cond/branch_18_fun/pallas_call | solution.py:267
  69.5 1.8 %collective-permute-start.4 = (f32[17,1536]{1,0:T(8,128)S(1)}, f32[17,1536]{1,0:T(8,128)S(1)}, u32[]{:S(2)}, u32[]{:S(2)}) collective-permute-start(f32[17,1536]{1,0:T(8,128)S(1)} %broadcast_select_fusion.2), channel_id=1, source_target_pairs={{0,4},{2,6},{4,0},{6,2},{8,12},{10,14},{12,8},{14,10},{16,20},{18,... | collective-permute-start | bytes 313352 | tf_op jit(solution)/shard_map/ppermute | solution.py:369
  71.3 0.0 collective-permute-start.3
  71.3 5.2 %collective-permute-done.4 = f32[17,1536]{1,0:T(8,128)S(1)} collective-permute-done((f32[17,1536]{1,0:T(8,128)S(1)}, f32[17,1536]{1,0:T(8,128)S(1)}, u32[]{:S(2)}, u32[]{:S(2)}) %collective-permute-start.4) | collective-permute-done | bytes 104480 | tf_op jit(solution)/shard_map/ppermute | solution.py:369
  76.5 1.3 %collective-permute-start.5 = (f32[17,1536]{1,0:T(8,128)S(1)}, f32[17,1536]{1,0:T(8,128)S(1)}, u32[]{:S(2)}, u32[]{:S(2)}) collective-permute-start(f32[17,1536]{1,0:T(8,128)S(1)} %select_add_fusion), channel_id=1, source_target_pairs={{0,2},{2,0},{4,6},{6,4},{8,10},{10,8},{12,14},{14,12},{16,18},{18,... | collective-permute-start | bytes 313352 | tf_op jit(solution)/shard_map/ppermute | solution.py:371
  79.2 0.0 collective-permute-done.3
  79.2 0.0 collective-permute-done.5
  79.2 0.0 copy-done
  79.2 0.7 multiply_add_fusion
  (4 shorter events, 0.1 us)
Async XLA Ops:
  1.9 7.4 %collective-permute-start = (f32[49,1536]{1,0:T(8,128)S(1)}, f32[49,1536]{1,0:T(8,128)S(1)}, u32[]{:S(2)}, u32[]{:S(2)}) collective-permute-start(f32[49,1536]{1,0:T(8,128)S(1)} %constant_dynamic-update-slice_fusion.mine), channel_id=1, source_target_pairs={{0,2},{2,0},{4,6},{6,4},{8,10},{10,8},{12,14},{14,12},{16,18},{18,... | collective-permute-start | bytes 903176 | tf_op jit(solution)/shard_map/ppermute | solution.py:358
  5.2 9.6 %collective-permute-start.2 = (f32[49,1536]{1,0:T(8,128)S(1)}, f32[49,1536]{1,0:T(8,128)S(1)}, u32[]{:S(2)}, u32[]{:S(2)}) collective-permute-start(f32[49,1536]{1,0:T(8,128)S(1)} %constant_dynamic-update-slice_fusion.mine), channel_id=1, source_target_pairs={{0,1},{1,0},{2,3},{3,2},{4,5},{5,4},{6,7},{7,6},{8,9},{9,8},{10,11... | collective-permute-start | bytes 903176 | tf_op jit(solution)/shard_map/ppermute | solution.py:359
  9.3 13.6 %collective-permute-start.1 = (f32[49,1536]{1,0:T(8,128)S(1)}, f32[49,1536]{1,0:T(8,128)S(1)}, u32[]{:S(2)}, u32[]{:S(2)}) collective-permute-start(f32[49,1536]{1,0:T(8,128)S(1)} %broadcast_select_fusion), channel_id=1, source_target_pairs={{0,4},{2,6},{4,0},{6,2},{8,12},{10,14},{12,8},{14,10},{16,20},{18,... | collective-permute-start | bytes 903176 | tf_op jit(solution)/shard_map/ppermute | solution.py:361
  23.0 56.2 %copy-start = (f32[17,1536]{1,0:T(8,128)S(1)}, f32[17,1536]{1,0:T(8,128)}, u32[]{:S(2)}) copy-start(f32[17,1536]{1,0:T(8,128)} %param.39) | copy-start | bytes 313348
  69.5 7.0 %collective-permute-start.4 = (f32[17,1536]{1,0:T(8,128)S(1)}, f32[17,1536]{1,0:T(8,128)S(1)}, u32[]{:S(2)}, u32[]{:S(2)}) collective-permute-start(f32[17,1536]{1,0:T(8,128)S(1)} %broadcast_select_fusion.2), channel_id=1, source_target_pairs={{0,4},{2,6},{4,0},{6,2},{8,12},{10,14},{12,8},{14,10},{16,20},{18,... | collective-permute-start | bytes 313352 | tf_op jit(solution)/shard_map/ppermute | solution.py:369
  71.3 7.9 %collective-permute-start.3 = (f32[17,1536]{1,0:T(8,128)S(1)}, f32[17,1536]{1,0:T(8,128)S(1)}, u32[]{:S(2)}, u32[]{:S(2)}) collective-permute-start(f32[17,1536]{1,0:T(8,128)S(1)} %get-tuple-element.796), channel_id=1, source_target_pairs={{0,1},{1,0},{2,3},{3,2},{4,5},{5,4},{6,7},{7,6},{8,9},{9,8},{10,11... | collective-permute-start | bytes 313352 | tf_op jit(solution)/shard_map/ppermute | solution.py:368
  76.5 2.6 %collective-permute-start.5 = (f32[17,1536]{1,0:T(8,128)S(1)}, f32[17,1536]{1,0:T(8,128)S(1)}, u32[]{:S(2)}, u32[]{:S(2)}) collective-permute-start(f32[17,1536]{1,0:T(8,128)S(1)} %select_add_fusion), channel_id=1, source_target_pairs={{0,2},{2,0},{4,6},{6,4},{8,10},{10,8},{12,14},{14,12},{16,18},{18,... | collective-permute-start | bytes 313352 | tf_op jit(solution)/shard_map/ppermute | solution.py:371

commit v4 on v3

--- a/solution.py
+++ b/solution.py
@@ -163,14 +163,16 @@
     barrier = pltpu.get_barrier_semaphore()
     for device in (to, sender):
         pl.semaphore_signal(barrier, inc=1, device_id=device, device_id_type=MESH)
-    fetch = pltpu.make_async_remote_copy(
-        src_ref=sent,
-        dst_ref=land.at[2],
-        send_sem=sems.at[0],
-        recv_sem=sems.at[1],
-        device_id=to,
-        device_id_type=MESH,
-    )
+    def fetch(i):
+        c = column_step(i)
+        return pltpu.make_async_remote_copy(
+            src_ref=sent.at[:, c],
+            dst_ref=land.at[2, :, c],
+            send_sem=sems.at[0, i],
+            recv_sem=sems.at[1, i],
+            device_id=to,
+            device_id_type=MESH,
+        )
 
     def give(i):
         c = pl.ds(pl.multiple_of(i * COLUMNS, COLUMNS), COLUMNS)
@@ -218,11 +220,16 @@
         @pl.when(i == GREETED)
         def _():
             pl.semaphore_wait(barrier, 2)
-            fetch.start()
-
-        @pl.when(i == 2 * first)
+
+            def begin(k, carry):
+                fetch(k).start()
+                return carry
+
+            lax.fori_loop(0, steps, begin, 0)
+
+        @pl.when(visit + 2 - slot == 0)
         def _():
-            fetch.wait()
+            fetch(at).wait()
 
         @pl.when(visit == 0)
         def _():
@@ -281,7 +288,7 @@
             pltpu.VMEM((ROWS, COLUMNS), F32),
             pltpu.VMEM((ROWS, COLUMNS), BF16),
             pltpu.VMEM((ROWS, COLUMNS), LOW),
-            pltpu.SemaphoreType.DMA((2,)),
+            pltpu.SemaphoreType.DMA((2, steps)),
             pltpu.SemaphoreType.DMA((2, steps)),
         ],
         cost_estimate=estimate(n, 80),

time: 80.9 us -> 81.8 us (1.011)
  starting transfers between devices: 8.73 us -> 11.1 us
  waiting for transfers between devices: 8.66 us -> 7.41 us
    ppermute x1, starting transfers between devices: 1.33 us -> 3.94 us  [local(): lax.ppermute(for_beside + jnp.where(lent_chip, kept, 0.0), 'blk', chip)]
    ppermute x1, waiting for transfers between devices: 5.25 us -> 3.99 us  [local(): from_across = lax.ppermute(jnp.where(lent_far, returned, 0.0), 'blk', apart)]
where the time goes in v4:
time: 81.8 us; the launch traced here: 81.3 us
  Pallas kernels  54.2 us (66%)
  starting transfers between devices  11.1 us (14%)
  waiting for transfers between devices  7.41 us (9%)
  local copies, waits for them, and re-layouts  3.42 us (4%)
  between operations  3.31 us (4%)
  other arithmetic  1.49 us (2%)
    pallas_call x1, Pallas kernels, rounds(): pl.pallas_call(functools.partial(rounds_body, route=route), out_shape=(ja...  46.3 us
    pallas_call x1, Pallas kernels, one_way(): pl.pallas_call(one_way_body, out_shape=(jax.ShapeDtypeStruct((17, n), F32...  7.91 us
    ppermute x1, waiting for transfers between devices, local(): from_across = lax.ppermute(jnp.where(lent_far, returned, 0.0), 'blk', apart)  3.99 us
    ppermute x1, starting transfers between devices, local(): lax.ppermute(for_beside + jnp.where(lent_chip, kept, 0.0), 'blk', chip)  3.94 us
    ppermute x1, starting transfers between devices, local(): beside = lax.ppermute(mine, 'blk', chip)  3.33 us
    ppermute x1, waiting for transfers between devices, local(): sibling = lax.ppermute(mine, 'half', swap)  3.22 us
    ppermute x1, starting transfers between devices, local(): across = lax.ppermute(lent, 'blk', apart)  2.28 us
  transfers between devices with their start and end apart: 6, of which 3 were waited for; matrix products, arithmetic and copies ran while one was open for 3% of the time, Pallas kernels for 10%

profile of v4, /device:TPU:1, one launch (start us, length us, event | category | flops | bytes accessed | tf_op | source)
XLA Modules:
  0.0 81.3 jit_solution(14891901818482112095)
XLA Ops:
  0.0 0.9 %constant_dynamic-update-slice_fusion.1 = f32[49,1536]{1,0:T(8,128)S(1)} fusion(f32[32,1536]{1,0:T(8,128)} %param.38), kind=kLoop, calls=%fused_computation.7 | loop fusion | bytes 393216
  0.9 0.9 %constant_dynamic-update-slice_fusion.mine = f32[49,1536]{1,0:T(8,128)S(1)} fusion(f32[49,1536]{1,0:T(8,128)S(1)} %constant_dynamic-update-slice_fusion.1, f32[17,1536]{1,0:T(8,128)} %param.39), kind=kLoop, calls=%fused_computation.6 | loop fusion | bytes 251904 | tf_op jit(solution)/shard_map/concatenate | solution.py:347
  1.9 3.3 %collective-permute-start = (f32[49,1536]{1,0:T(8,128)S(1)}, f32[49,1536]{1,0:T(8,128)S(1)}, u32[]{:S(2)}, u32[]{:S(2)}) collective-permute-start(f32[49,1536]{1,0:T(8,128)S(1)} %constant_dynamic-update-slice_fusion.mine), channel_id=1, source_target_pairs={{0,2},{2,0},{4,6},{6,4},{8,10},{10,8},{12,14},{14,12},{16,18},{18,... | collective-permute-start | bytes 903176 | tf_op jit(solution)/shard_map/ppermute | solution.py:365
  5.2 0.0 collective-permute-start.2
  5.2 1.4 %fusion = (s32[1]{0:T(128)}, s32[1]{0:T(128)}, s32[1]{0:T(128)}) fusion(s32[3]{0:T(128)} %param.43), kind=kLoop, calls=%fused_computation.9 | loop fusion | bytes 24 | tf_op jit(solution)/shard_map/slice | solution.py:350
  8.5 0.7 multiply_bitcast_fusion
  9.2 0.1 copy.7.inv
  9.3 0.0 collective-permute-done
  9.3 2.3 %collective-permute-start.1 = (f32[49,1536]{1,0:T(8,128)S(1)}, f32[49,1536]{1,0:T(8,128)S(1)}, u32[]{:S(2)}, u32[]{:S(2)}) collective-permute-start(f32[49,1536]{1,0:T(8,128)S(1)} %broadcast_select_fusion), channel_id=1, source_target_pairs={{0,4},{2,6},{4,0},{6,2},{8,12},{10,14},{12,8},{14,10},{16,20},{18,... | collective-permute-start | bytes 903176 | tf_op jit(solution)/shard_map/ppermute | solution.py:368
  11.6 3.2 %collective-permute-done.2.sibling = f32[49,1536]{1,0:T(8,128)S(1)} collective-permute-done((f32[49,1536]{1,0:T(8,128)S(1)}, f32[49,1536]{1,0:T(8,128)S(1)}, u32[]{:S(2)}, u32[]{:S(2)}) %collective-permute-start.2) | collective-permute-done | bytes 301088 | tf_op jit(solution)/shard_map/ppermute | solution.py:366
  14.8 7.9 %shard_map.64 = (f32[17,1536]{1,0:T(8,128)}, bf16[2,1536,256]{2,1,0:T(8,128)(2,1)S(1)}, bf16[2,48,1536]{2,1,0:T(8,128)(2,1)}, f8e5m2[2,64,1536]{2,1,0:T(32,128)(4,1)S(1)}) custom-call(f32[49,1536]{1,0:T(8,128)S(1)} %constant_dynamic-update-slice_fusion.mine, f32[49,1536]{1,0:T(8,128)S(1)} %collective-permute-done.2.sibling, f32[32,1]{1,0:T(8,128)S(1)} %copy.7.inv), custom_call_target="tpu_custom_call" | custom-call | flops 12079595520 | bytes 706560 | tf_op jit(solution)/shard_map/pallas_call | solution.py:129
  22.7 0.2 collective-permute-done.1
  23.0 0.0 copy-start
  23.0 46.7 %conditional.1 = ((f32[17,1536]{1,0:T(8,128)S(1)}, f32[17,1536]{1,0:T(8,128)S(1)}, f32[17,1536]{1,0:T(8,128)S(1)}, f32[17,1536]{1,0:T(8,128)S(1)})) conditional(s32[]{:T(128)} %bitcast.1, (f32[49,1536]{1,0:T(8,128)S(1)}, f32[49,1536]{1,0:T(8,128)S(1)}, f32[49,1536]{1,0:T(8,128)S(1)}, f32[32,1]{0,1:T(1,128)S(1)}, ...), branch_computations={%region_0.1_spmd, %region_1.2_spmd, %region_2.3_spmd, %region_3.4_... | conditional | flops 96636764160 | bytes 706824 | solution.py:374
  23.2 0.1 copy.27.inv
  23.3 46.3 %branch_19_fun.1 = (f32[17,1536]{1,0:T(8,128)S(1)}, f32[17,1536]{1,0:T(8,128)S(1)}, f32[17,1536]{1,0:T(8,128)S(1)}, f32[17,1536]{1,0:T(8,128)S(1)}) custom-call(f32[49,1536]{1,0:T(8,128)S(1)} %get-tuple-element.669.sent, f32[49,1536]{1,0:T(8,128)S(1)} %get-tuple-element.670.beside, f32[49,1536]{1,0:T(8,128)S(1)} %get-tuple-element.671.mine, ...), custom_call_target="tpu_custom_call" | custom-call | flops 96636764160 | bytes 706560 | tf_op jit(solution)/shard_map/cond/branch_19_fun/pallas_call | solution.py:274
  69.7 1.6 %collective-permute-start.4 = (f32[17,1536]{1,0:T(8,128)S(1)}, f32[17,1536]{1,0:T(8,128)S(1)}, u32[]{:S(2)}, u32[]{:S(2)}) collective-permute-start(f32[17,1536]{1,0:T(8,128)S(1)} %broadcast_select_fusion.2), channel_id=1, source_target_pairs={{0,4},{2,6},{4,0},{6,2},{8,12},{10,14},{12,8},{14,10},{16,20},{18,... | collective-permute-start | bytes 313352 | tf_op jit(solution)/shard_map/ppermute | solution.py:376
  71.2 0.0 collective-permute-start.3
  71.3 4.0 %collective-permute-done.4 = f32[17,1536]{1,0:T(8,128)S(1)} collective-permute-done((f32[17,1536]{1,0:T(8,128)S(1)}, f32[17,1536]{1,0:T(8,128)S(1)}, u32[]{:S(2)}, u32[]{:S(2)}) %collective-permute-start.4) | collective-permute-done | bytes 104480 | tf_op jit(solution)/shard_map/ppermute | solution.py:376
  75.3 3.9 %collective-permute-start.5 = (f32[17,1536]{1,0:T(8,128)S(1)}, f32[17,1536]{1,0:T(8,128)S(1)}, u32[]{:S(2)}, u32[]{:S(2)}) collective-permute-start(f32[17,1536]{1,0:T(8,128)S(1)} %select_add_fusion), channel_id=1, source_target_pairs={{0,2},{2,0},{4,6},{6,4},{8,10},{10,8},{12,14},{14,12},{16,18},{18,... | collective-permute-start | bytes 313352 | tf_op jit(solution)/shard_map/ppermute | solution.py:378
  80.5 0.0 collective-permute-done.3
  80.5 0.0 collective-permute-done.5
  80.5 0.0 copy-done
  80.5 0.7 multiply_add_fusion
  (4 shorter events, 0.1 us)
Async XLA Ops:
  1.9 7.4 %collective-permute-start = (f32[49,1536]{1,0:T(8,128)S(1)}, f32[49,1536]{1,0:T(8,128)S(1)}, u32[]{:S(2)}, u32[]{:S(2)}) collective-permute-start(f32[49,1536]{1,0:T(8,128)S(1)} %constant_dynamic-update-slice_fusion.mine), channel_id=1, source_target_pairs={{0,2},{2,0},{4,6},{6,4},{8,10},{10,8},{12,14},{14,12},{16,18},{18,... | collective-permute-start | bytes 903176 | tf_op jit(solution)/shard_map/ppermute | solution.py:365
  5.2 9.6 %collective-permute-start.2 = (f32[49,1536]{1,0:T(8,128)S(1)}, f32[49,1536]{1,0:T(8,128)S(1)}, u32[]{:S(2)}, u32[]{:S(2)}) collective-permute-start(f32[49,1536]{1,0:T(8,128)S(1)} %constant_dynamic-update-slice_fusion.mine), channel_id=1, source_target_pairs={{0,1},{1,0},{2,3},{3,2},{4,5},{5,4},{6,7},{7,6},{8,9},{9,8},{10,11... | collective-permute-start | bytes 903176 | tf_op jit(solution)/shard_map/ppermute | solution.py:366
  9.3 13.6 %collective-permute-start.1 = (f32[49,1536]{1,0:T(8,128)S(1)}, f32[49,1536]{1,0:T(8,128)S(1)}, u32[]{:S(2)}, u32[]{:S(2)}) collective-permute-start(f32[49,1536]{1,0:T(8,128)S(1)} %broadcast_select_fusion), channel_id=1, source_target_pairs={{0,4},{2,6},{4,0},{6,2},{8,12},{10,14},{12,8},{14,10},{16,20},{18,... | collective-permute-start | bytes 903176 | tf_op jit(solution)/shard_map/ppermute | solution.py:368
  23.0 57.6 %copy-start = (f32[17,1536]{1,0:T(8,128)S(1)}, f32[17,1536]{1,0:T(8,128)}, u32[]{:S(2)}) copy-start(f32[17,1536]{1,0:T(8,128)} %param.39) | copy-start | bytes 313348
  69.7 5.6 %collective-permute-start.4 = (f32[17,1536]{1,0:T(8,128)S(1)}, f32[17,1536]{1,0:T(8,128)S(1)}, u32[]{:S(2)}, u32[]{:S(2)}) collective-permute-start(f32[17,1536]{1,0:T(8,128)S(1)} %broadcast_select_fusion.2), channel_id=1, source_target_pairs={{0,4},{2,6},{4,0},{6,2},{8,12},{10,14},{12,8},{14,10},{16,20},{18,... | collective-permute-start | bytes 313352 | tf_op jit(solution)/shard_map/ppermute | solution.py:376
  71.2 9.3 %collective-permute-start.3 = (f32[17,1536]{1,0:T(8,128)S(1)}, f32[17,1536]{1,0:T(8,128)S(1)}, u32[]{:S(2)}, u32[]{:S(2)}) collective-permute-start(f32[17,1536]{1,0:T(8,128)S(1)} %get-tuple-element.796), channel_id=1, source_target_pairs={{0,1},{1,0},{2,3},{3,2},{4,5},{5,4},{6,7},{7,6},{8,9},{9,8},{10,11... | collective-permute-start | bytes 313352 | tf_op jit(solution)/shard_map/ppermute | solution.py:375
  75.3 5.2 %collective-permute-start.5 = (f32[17,1536]{1,0:T(8,128)S(1)}, f32[17,1536]{1,0:T(8,128)S(1)}, u32[]{:S(2)}, u32[]{:S(2)}) collective-permute-start(f32[17,1536]{1,0:T(8,128)S(1)} %select_add_fusion), channel_id=1, source_target_pairs={{0,2},{2,0},{4,6},{6,4},{8,10},{10,8},{12,14},{14,12},{16,18},{18,... | collective-permute-start | bytes 313352 | tf_op jit(solution)/shard_map/ppermute | solution.py:378
